TPU v7x, 256 devices: a whole 4x4x8 slice. The times are simulated.
256 devices in a mesh: dp: 32 (over z, y), tensor: 8 (over x, core).
Axes of the slice: x: 4, y: 4, z: 8, core: 2. Of those that a mesh axis runs over, the one named last changes fastest.
Arguments:
- gradients: bfloat16 [32, 64, 512, 512], P('dp', 'tensor')
- owners: int32 [8, 32], P('tensor'), may hold values from 0 to 31, each once within a row
- left_factor: float32 [8, 32, 512, 512], P('tensor', 'dp')
- right_factor: float32 [8, 32, 512, 512], P('tensor', 'dp')
- left_root: bfloat16 [8, 32, 512, 512], P('tensor', 'dp')
- right_root: bfloat16 [8, 32, 512, 512], P('tensor', 'dp')
Outputs:
- new_left: float32 [8, 32, 512, 512], P('tensor', 'dp')
- new_right: float32 [8, 32, 512, 512], P('tensor', 'dp')
- directions: bfloat16 [64, 512, 512], P('tensor', 'dp')
Inputs may be any that keep to these rules, and one draw needn't show every extreme that they name: Each row of owners is a permutation of the replica indices; block j < 8 of tensor shard t is owned by replica owners[t, j], the replicas in the other entries own no block.
All inputs are finite; a program needn't handle non-finite values.
Results may differ from a plain program's by a relative error of at most 0.025.
Values may be sent and summed in bfloat16 or wider, within the bound.
A program may use at most 128 MiB of HBM per device.

v0:
```python
import jax
import jax.numpy as jnp
from jax import lax
from jax.sharding import PartitionSpec as P

decay_rate = 0.95
epsilon = 1e-06


def per_device(gradients, owners, left_factor, right_factor, left_root, right_root):
    blocks = gradients[0]
    block_total = blocks.shape[0]
    block_width = blocks.shape[1]
    peer_count = lax.axis_size("dp")
    strip_rows = block_width // peer_count
    row_start = lax.axis_index("dp") * strip_rows
    held_by = owners[0, :block_total]
    slot_ids = lax.iota(jnp.int32, 1 * lax.axis_size("dp"))
    select = (held_by[None, :] == slot_ids[:, None]).astype(jnp.bfloat16)
    grad_sum = lax.psum_scatter(
        jnp.einsum("sn,nab->sab", select, blocks, preferred_element_type=jnp.float32).astype(
            jnp.bfloat16
        ),
        "dp",
        scatter_dimension=0,
        tiled=True,
    ).astype(jnp.float32)[0]
    grad_block = grad_sum.astype(jnp.bfloat16)
    gram_weight = (1.0 - decay_rate) / block_width
    left_gram = jnp.dot(grad_block, grad_block.T, preferred_element_type=jnp.float32)
    right_gram = jnp.dot(grad_block.T, grad_block, preferred_element_type=jnp.float32)
    new_left = decay_rate * left_factor[0, 0] + gram_weight * left_gram
    new_right = decay_rate * right_factor[0, 0] + gram_weight * right_gram
    half_way = jnp.dot(left_root[0, 0], grad_block, preferred_element_type=jnp.float32).astype(
        jnp.bfloat16
    )
    precond = jnp.dot(half_way, right_root[0, 0], preferred_element_type=jnp.float32)
    shaped = (
        precond
        * jnp.sqrt(jnp.mean(grad_sum * grad_sum) + epsilon)
        / jnp.sqrt(jnp.mean(precond * precond) + epsilon)
    )
    local_sum = jnp.sum(shaped * shaped)
    global_sum = lax.psum(local_sum, ("dp", "tensor"))
    entry_total = block_total * lax.axis_size("tensor") * block_width * block_width
    scale = 1.0 / jnp.sqrt(global_sum / entry_total + epsilon)
    scaled = (shaped * scale).astype(jnp.bfloat16)
    gathered = lax.all_gather(scaled[None], "dp", axis=0, tiled=True)
    my_rows = lax.dynamic_slice_in_dim(gathered, row_start, strip_rows, 1)
    peer_ids = lax.iota(jnp.int32, peer_count)
    choose = (held_by[:, None] == peer_ids[None, :]).astype(jnp.bfloat16)
    directions = jnp.einsum(
        "np,pab->nab", choose, my_rows, preferred_element_type=jnp.float32
    ).astype(jnp.bfloat16)
    return (new_left[None, None], new_right[None, None], directions)


def solution(mesh):
    return jax.shard_map(
        per_device,
        mesh=mesh,
        in_specs=(
            P("dp", "tensor", None, None),
            P("tensor", None),
            P("tensor", "dp", None, None),
            P("tensor", "dp", None, None),
            P("tensor", "dp", None, None),
            P("tensor", "dp", None, None),
        ),
        out_specs=(
            P("tensor", "dp", None, None),
            P("tensor", "dp", None, None),
            P("tensor", "dp", None),
        ),
        check_vma=False,
    )
```

profile of v0, /device:TPU:32, one launch (start us, length us, event | category | flops | bytes accessed | tf_op | source)
XLA Modules:
  0.0 510.0 jit_solution(12893641419845845962)
XLA Ops:
  7.2 0.0 copy-start
  7.2 0.0 reduce-scatter.2.cloned.1.call-start
  7.2 0.7 slice_bitcast_fusion
  7.9 9.9 %convolution_convert_fusion = bf16[32,512,512]{2,0,1:T(8,128)(2,1)} fusion(bf16[8,512,512]{2,1,0:T(8,128)(2,1)} %bitcast.39, s32[8]{0:T(128)S(1)} %slice_bitcast_fusion), kind=kOutput, calls=%fused_computation | convolution fusion | flops 142606592 | bytes 20971552 | tf_op jit(solution)/shard_map/sn,nab->sab/dot_general | solution.py:21
  17.8 16.8 %copy.16 = bf16[32,512,512]{2,1,0:T(8,128)(2,1)} copy(bf16[32,512,512]{2,0,1:T(8,128)(2,1)} %convolution_convert_fusion) | data formatting | bytes 33554432 | tf_op jit(solution)/shard_map/convert_element_type | solution.py:21
  34.6 0.0 copy-start.2
  34.6 0.0 reduce-scatter.2.cloned.1.call-update
  34.7 0.0 all-gather.3.cloned.1.call-start
  34.7 247.0 %reduce-scatter.2.cloned.1.call-done = bf16[1,512,512]{2,1,0:T(8,128)(2,1)} async-done(((bf16[32,512,512]{2,1,0:T(8,128)(2,1)}), bf16[1,512,512]{2,1,0:T(8,128)(2,1)}) %reduce-scatter.2.cloned.1.call-update) | async-done | bytes 524304 | tf_op jit(solution)/shard_map/reduce_scatter | solution.py:20
  281.8 0.0 copy-done
  281.8 0.0 copy-done.2
  281.8 2.7 multiply_reduce_fusion.1
  285.1 1.9 multiply_reduce_fusion.2
  287.7 0.9 multiply_reduce_fusion
  288.6 75.0 %psum.7 = f32[]{:T(128)} all-reduce(f32[]{:T(128)} %multiply_reduce_fusion), channel_id=1, replica_groups=mesh['dp'=32,'tensor'=8] {'dp','tensor'}, use_global_device_ids=true, to_apply=%region_4.0 | all-reduce | flops 1 | bytes 8 | tf_op jit(solution)/shard_map/psum | solution.py:44
  364.3 0.9 multiply_convert_fusion
  365.2 0.0 all-gather.3.cloned.1.call-update
  365.3 0.0 copy-done.1
  365.3 2.7 fusion.4
  367.9 3.0 fusion.2
  370.9 130.1 %all-gather.3.cloned.1.call-done = bf16[16384,512]{1,0:T(8,128)(2,1)} async-done(((bf16[512,512]{1,0:T(8,128)(2,1)}), bf16[16384,512]{1,0:T(8,128)(2,1)}) %all-gather.3.cloned.1.call-update) | async-done | bytes 16777232 | tf_op jit(solution)/shard_map/all_gather | solution.py:48
  501.0 1.1 constant_dynamic-slice_fusion
  502.1 0.4 convolution_convert_fusion.2
  502.5 0.7 copy.18
  (1 shorter events, 0.0 us)
Async XLA Ops:
  7.2 274.6 %copy-start = (bf16[1,1,512,512]{3,2,1,0:T(8,128)(2,1)S(1)}, bf16[1,1,512,512]{3,2,1,0:T(8,128)(2,1)}, u32[]{:S(2)}) copy-start(bf16[1,1,512,512]{3,2,1,0:T(8,128)(2,1)} %param.11) | copy-start | bytes 1572868
  7.2 274.6 %reduce-scatter.2.cloned.1.call-start = ((), (), s32[]{:S(2)}) async-start(), calls=%async_computation.1 | async-start | bytes 17301504 | tf_op jit(solution)/shard_map/reduce_scatter | solution.py:20
  34.6 247.1 %copy-start.2 = (bf16[1,1,512,512]{3,2,1,0:T(8,128)(2,1)S(1)}, bf16[1,1,512,512]{3,2,1,0:T(8,128)(2,1)}, u32[]{:S(2)}) copy-start(bf16[1,1,512,512]{3,2,1,0:T(8,128)(2,1)} %param.10) | copy-start | bytes 1572868
  34.6 330.6 %copy-start.1 = (f32[1,1,512,512]{3,2,1,0:T(8,128)S(1)}, f32[1,1,512,512]{3,2,1,0:T(8,128)}, u32[]{:S(2)}) copy-start(f32[1,1,512,512]{3,2,1,0:T(8,128)} %param.8) | copy-start | bytes 3145732
  34.7 466.4 %all-gather.3.cloned.1.call-start = ((), (), s32[]{:S(2)}) async-start(), calls=%async_computation.2 | async-start | bytes 17301504 | tf_op jit(solution)/shard_map/all_gather | solution.py:48
Sparse Core Ops, SparseCore 0:
  34.8 246.9 reduce-scatter.1
  365.4 135.5 all-gather.2
where the time goes:
time: 513 us; the launch traced here: 510 us
  waiting for transfers between devices  377 us (73%)
  blocking collectives  75 us (15%)
  local copies, waits for them, and re-layouts  19.3 us (4%)
  matrix products  18.6 us (4%)
  between operations  16.2 us (3%)
    reduce_scatter x1, waiting for transfers between devices, per_device(): lax.psum_scatter(jnp.einsum('sn,nab->sab', select, blocks, preferred_elem...  247 us
    all_gather x1, waiting for transfers between devices, per_device(): gathered = lax.all_gather(scaled[None], 'dp', axis=0, tiled=True)  130 us
    psum x1, blocking collectives, per_device(): global_sum = lax.psum(local_sum, ('dp', 'tensor'))  75 us
    convert_element_type x1, local copies, waits for them, and re-layouts, per_device(): jnp.einsum('sn,nab->sab', select, blocks, preferred_element_type=jnp.floa...  16.8 us
  transfers between devices with their start and end apart: 2, of which 2 were waited for; matrix products, arithmetic and copies ran while one was open for 1% of the time, Pallas kernels for 0%

commit v1 on v0

v1 whole, which is shorter than its diff:
```python
import functools

import jax
import jax.numpy as jnp
from jax import lax
from jax.experimental import pallas as pl
from jax.experimental.pallas import tpu as pltpu
from jax.sharding import PartitionSpec as P

MESH = pl.DeviceIdType.MESH
F32 = jnp.float32
BF16 = jnp.bfloat16
decay_rate = 0.95
epsilon = 1e-06
NY = 4

ROUNDS = (
    (0, 256, (3, 3, 1, 1)),
    (256, 256, (3, 2, 1, 2)),
)


def sets_of(counts):
    at, found = 0, []
    for nb, (yfirst, s) in zip(counts, ((True, 1), (True, -1), (False, 1), (False, -1))):
        if nb:
            found.append((at, nb, yfirst, s))
        at += nb
    return found


def plan(events, rate=0.18, latency=1.5, lead=2.0):
    free = dict.fromkeys(("y1", "y-1", "z1", "z-1"), 0.0)
    arrive, done, order, now = {}, {}, [], 0.0
    left = list(events)
    while left:
        best = None
        for e in left:
            if any(m not in arrive for m in e["needs"]) or any(d not in done for d in e["after"]):
                continue
            ready = max([arrive[m] for m in e["needs"]] + [now])
            if not e["needs"] and not e["after"]:
                ready = max([now] + [free[link] - lead for _, link, _ in e["sends"]])
            key = (ready, e["rank"])
            if best is None or key < best[0]:
                best = (key, e)
        (ready, _), e = best
        now = ready + e["cost"]
        for name, link, kib in e["sends"]:
            free[link] = max(free[link], now) + kib * 1.024 / 100 * 2 / 0.9
            arrive[name] = free[link] + latency
        done[e["name"]] = now
        order.append(e)
        left.remove(e)
    return order, now


def per_device(nz, n_tensor, gradients, owners, left_factor, right_factor, left_root, right_root):
    nb_all, width = gradients.shape[1], gradients.shape[2]
    n_dp = nz * NY
    strip = width // n_dp
    g = gradients.reshape(nb_all, nz, NY, strip, width)
    sets = [(k, c0, w) + s for k, (c0, w, counts) in enumerate(ROUNDS) for s in sets_of(counts)]
    names, shapes = [], []

    def buffer(name, shape, dtype=BF16):
        names.append(name)
        shapes.append(pltpu.VMEM(shape, dtype))

    messages = {}
    for i, (k, c0, w, b0, nb, yfirst, s) in enumerate(sets):
        ychunk = (nb, nz, strip, w) if yfirst else (nb, strip, w)
        zchunk = (nb, strip, w) if yfirst else (nb, NY, strip, w)
        for n in ("ry1", "ry2", "ry3", "sy"):
            buffer(f"{n}_{i}", ychunk)
        buffer(f"mid_{i}", ychunk if yfirst else zchunk)
        half = nz // 2
        buffer(f"rza_{i}", (half,) + zchunk)
        buffer(f"rzb_{i}", (half - 1,) + zchunk)
        buffer(f"sza_{i}", (half - 1,) + zchunk)
        buffer(f"szb_{i}", (half - 2,) + zchunk)
        for n in ["y1", "y2", "y3"] + [f"a{h}" for h in range(half)] + [f"b{h}" for h in range(half - 1)]:
            messages[f"{n}_{i}"] = len(messages)
    for k, (c0, w, _) in enumerate(ROUNDS):
        buffer(f"agg_{k}", (nb_all, strip, w))
        buffer(f"stage_{k}", (n_dp, strip, w))
        buffer(f"grad_{k}", (n_dp, strip, w))
    buffer("own", (nb_all, nz, NY, strip, width))
    buffer("lroot", (width, width))
    buffer("rroot", (width, width))
    buffer("lfac", (width, width), F32)
    buffer("rfac", (width, width), F32)
    buffer("pre", (width, width), F32)
    buffer("shaped", (n_dp, strip, width))
    buffer("arrived", (n_dp, strip, width))
    buffer("sum_t", (n_tensor, 8, 128), F32)
    buffer("sum_y", (NY, 8, 128), F32)
    buffer("sum_z", (nz, 8, 128), F32)

    n_msg = len(messages)
    n_rounds = len(ROUNDS)

    def kernel(owners_ref, g_ref, lf_ref, rf_ref, lr_ref, rr_ref, nl_ref, nr_ref, dir_ref, *scratch):
        buf = dict(zip(names, scratch))
        send, recv, own_sem, load_sem, a2a_send, a2a_recv, sum_send, sum_recv, out_sem = scratch[len(names):]
        me, ten = lax.axis_index("dp"), lax.axis_index("tensor")
        z, y = me // NY, me % NY

        def zat(d):
            return lax.rem(z + d + 2 * nz, nz)

        def yat(d):
            return lax.rem(y + d + 2 * NY, NY)

        def zdev(d):
            return (zat(d) * NY + y, ten)

        def ydev(d):
            return (z * NY + yat(d), ten)

        barrier = pltpu.get_barrier_semaphore()

        def greet(o, _):
            pl.semaphore_signal(barrier, inc=1, device_id=(lax.rem(me + o, n_dp), ten), device_id_type=MESH)
            return 0

        lax.fori_loop(1, n_dp, greet, 0)
        for o in range(1, n_tensor):
            pl.semaphore_signal(barrier, inc=1, device_id=(me, lax.rem(ten + o, n_tensor)), device_id_type=MESH)
        pl.semaphore_wait(barrier, n_dp - 1 + n_tensor - 1)

        own_copies = []
        for k, (c0, w, _) in enumerate(ROUNDS):
            cols = pl.ds(c0, w)
            own_copies.append(
                pltpu.make_async_copy(
                    g_ref.at[:, :, :, :, cols], buf["own"].at[:, :, :, :, cols], own_sem.at[k]
                )
            )
        loads = [
            pltpu.make_async_copy(lr_ref, buf["lroot"], load_sem.at[0]),
            pltpu.make_async_copy(rr_ref, buf["rroot"], load_sem.at[1]),
            pltpu.make_async_copy(lf_ref, buf["lfac"], load_sem.at[2]),
            pltpu.make_async_copy(rf_ref, buf["rfac"], load_sem.at[3]),
        ]
        copies = {}

        def put(name, src, dst, dev):
            i = messages[name]
            copies[name] = pltpu.make_async_remote_copy(
                src_ref=src, dst_ref=dst, send_sem=send.at[i], recv_sem=recv.at[i],
                device_id=dev, device_id_type=MESH,
            )
            copies[name].start()

        def total(parts):
            if len(parts) == 2:
                return parts[0] + parts[1]
            acc = parts[0].astype(F32)
            for p in parts[1:]:
                acc = acc + p.astype(F32)
            return acc.astype(BF16)

        events = []

        def event(name, emit, rank, needs=(), after=(), sends=(), cost=0.2):
            events.append(dict(name=name, emit=emit, rank=rank, needs=needs, after=after, sends=sends, cost=cost))

        loaded = set()

        def need_own(k):
            if k not in loaded:
                loaded.add(k)
                own_copies[k].wait()

        half = nz // 2
        finals = {k: [] for k in range(n_rounds)}
        for i, (k, c0, w, b0, nb, yfirst, s) in enumerate(sets):
            cols = pl.ds(c0, w)
            blocks = pl.ds(b0, nb)
            kib = nb * strip * w * 2 / 1024

            def own_y(src, i=i, blocks=blocks, cols=cols, yfirst=yfirst):
                return (lambda d: src.at[blocks, :, yat(d), :, cols]) if yfirst else (lambda d: src.at[:, yat(d)])

            def own_z(src, i=i, blocks=blocks, cols=cols, yfirst=yfirst):
                return (lambda d: src.at[:, zat(d)]) if yfirst else (lambda d: src.at[blocks, zat(d), :, :, cols])

            def fold(dst, parts, lead, n_lead, nb=nb):
                if not lead:
                    for b in range(nb):
                        dst[b] = total([p[b] for p in parts])
                    return

                def one(v, _):
                    for b in range(nb):
                        dst[b, v] = total([p[b, v] for p in parts])
                    return 0

                lax.fori_loop(0, n_lead, one, 0)

            first_y, first_z = yfirst, not yfirst
            ysize = kib * nz if yfirst else kib
            zsize = kib if yfirst else kib * NY
            mid = buf[f"mid_{i}"]
            y_raw = own_y(g_ref if yfirst else mid)
            y_own = own_y(buf["own"] if yfirst else mid)
            z_raw = own_z(mid if yfirst else g_ref)
            z_own = own_z(mid if yfirst else buf["own"])
            agg = buf[f"agg_{k}"].at[blocks]
            ry1, ry2, ry3, sy = (buf[f"{n}_{i}"] for n in ("ry1", "ry2", "ry3", "sy"))
            rza, rzb, sza, szb = (buf[f"{n}_{i}"] for n in ("rza", "rzb", "sza", "szb"))
            ylead = (yfirst, nz)
            zlead = (not yfirst, NY)
            up, down = s, -s
            yl, zl = {1: f"y{s}", -1: f"y{-s}"}, {1: f"z{s}", -1: f"z{-s}"}
            yk = k * 10 + (0 if yfirst else 5)
            zk = k * 10 + (5 if yfirst else 0)
            ybase = () if yfirst else (f"zdone_{i}",)
            zbase = (f"ydone_{i}",) if yfirst else ()

            def y0(i=i, y_raw=y_raw, ry1=ry1, ry3=ry3, s=s):
                put(f"y1_{i}", y_raw(2 * s), ry1, ydev(s))
                put(f"y3_{i}", y_raw(-s), ry3, ydev(-s))

            def y1(i=i, k=k, y_own=y_own, ry1=ry1, ry2=ry2, sy=sy, s=s, fold=fold, ylead=ylead):
                need_own(k)
                copies[f"y1_{i}"].wait_recv()
                fold(sy, [ry1, y_own(s)], *ylead)
                put(f"y2_{i}", sy, ry2, ydev(s))

            def y2(i=i, k=k, y_own=y_own, ry2=ry2, ry3=ry3, fold=fold, ylead=ylead,
                   dst=mid if yfirst else agg):
                need_own(k)
                copies[f"y2_{i}"].wait_recv()
                copies[f"y3_{i}"].wait_recv()
                fold(dst, [ry2, ry3, y_own(0)], *ylead)

            event(f"y0_{i}", y0, yk, after=ybase,
                  sends=[(f"y1_{i}", yl[1], ysize), (f"y3_{i}", yl[-1], ysize)])
            event(f"y1_{i}", y1, yk - 1, needs=[f"y1_{i}"], sends=[(f"y2_{i}", yl[1], ysize)])
            event(f"ydone_{i}", y2, yk - 2, needs=[f"y2_{i}", f"y3_{i}"])

            def zstart(i=i, z_raw=z_raw, rza=rza, rzb=rzb, s=s):
                put(f"a0_{i}", z_raw(half * s), rza.at[0], zdev(s))
                put(f"b0_{i}", z_raw(-(half - 1) * s), rzb.at[0], zdev(-s))

            event(f"z0_{i}", zstart, zk, after=zbase,
                  sends=[(f"a0_{i}", zl[1], zsize), (f"b0_{i}", zl[-1], zsize)])
            for h in range(1, half):
                def za(i=i, k=k, h=h, z_own=z_own, rza=rza, sza=sza, s=s, fold=fold, zlead=zlead):
                    need_own(k)
                    copies[f"a{h - 1}_{i}"].wait_recv()
                    fold(sza.at[h - 1], [rza.at[h - 1], z_own((half - h) * s)], *zlead)
                    put(f"a{h}_{i}", sza.at[h - 1], rza.at[h], zdev(s))

                event(f"za{h}_{i}", za, zk - 1, needs=[f"a{h - 1}_{i}"], sends=[(f"a{h}_{i}", zl[1], zsize)])
            for h in range(1, half - 1):
                def zb(i=i, k=k, h=h, z_own=z_own, rzb=rzb, szb=szb, s=s, fold=fold, zlead=zlead):
                    need_own(k)
                    copies[f"b{h - 1}_{i}"].wait_recv()
                    fold(szb.at[h - 1], [rzb.at[h - 1], z_own(-(half - 1 - h) * s)], *zlead)
                    put(f"b{h}_{i}", szb.at[h - 1], rzb.at[h], zdev(-s))

                event(f"zb{h}_{i}", zb, zk - 1, needs=[f"b{h - 1}_{i}"], sends=[(f"b{h}_{i}", zl[-1], zsize)])

            def zend(i=i, k=k, z_own=z_own, rza=rza, rzb=rzb, fold=fold, zlead=zlead,
                     dst=agg if yfirst else mid):
                need_own(k)
                copies[f"a{half - 1}_{i}"].wait_recv()
                copies[f"b{half - 2}_{i}"].wait_recv()
                fold(dst, [rza.at[half - 1], rzb.at[half - 2], z_own(0)], *zlead)

            event(f"zdone_{i}", zend, zk - 2, needs=[f"a{half - 1}_{i}", f"b{half - 2}_{i}"])
            finals[k].append(f"zdone_{i}" if yfirst else f"ydone_{i}")

        def block_of(device):
            found = jnp.int32(0)
            for j in range(nb_all):
                found = jnp.where(owners_ref[0, j] == device, j, found)
            return found

        def peer(o):
            dz, dy = o // NY, o % NY
            step = jnp.where(dz % 2 == 1, (dz + 1) // 2, nz - dz // 2)
            return lax.rem(z + step, nz) * NY + lax.rem(y + dy, NY)

        for k, (c0, w, _) in enumerate(ROUNDS):
            kib = strip * w * 2 / 1024

            def route(k=k):
                agg, stage, grad = (buf[f"{n}_{k}"] for n in ("agg", "stage", "grad"))

                def one(o, _):
                    to = peer(o)
                    stage[o] = agg[block_of(to)]
                    pltpu.make_async_remote_copy(
                        src_ref=stage.at[o], dst_ref=grad.at[me], send_sem=a2a_send.at[k], recv_sem=a2a_recv.at[k],
                        device_id=(to, ten), device_id_type=MESH,
                    ).start()
                    return 0

                lax.fori_loop(1, n_dp, one, 0)
                grad[me] = agg[block_of(me)]

            event(f"route_{k}", route, k * 10 - 3, after=finals[k],
                  sends=[(f"rz{q}_{k}", f"z{q}", kib * 8 * NY) for q in (1, -1)]
                  + [(f"ry{q}_{k}", f"y{q}", kib * 2 * nz) for q in (1, -1)], cost=1.0)

        for c in own_copies:
            c.start()
        order, _ = plan(events)
        n_first = 0
        started = False
        for e in order:
            if not started and e["needs"]:
                started = True
                for c in loads:
                    c.start()
            e["emit"]()

        def a2a_all(sem, ref):
            part = ref.at[pl.ds(0, n_dp - 1)]
            return pltpu.make_async_copy(part, part, sem)

        for k in range(n_rounds):
            a2a_all(a2a_recv.at[k], buf[f"grad_{k}"]).wait()
        for c in loads:
            c.wait()

        def whole():
            parts = [buf[f"grad_{k}"][...].reshape(width, ROUNDS[k][1]) for k in range(n_rounds)]
            return parts[0] if len(parts) == 1 else jnp.concatenate(parts, axis=1)

        owned = jnp.int32(0)
        for j in range(nb_all):
            owned = owned + jnp.where(owners_ref[0, j] == me, 1, 0)
        mine = owned > 0
        grad = whole()
        tall = 128
        pre = buf["pre"]
        squares = jnp.zeros((8, width), F32)
        for i in range(width // tall):
            rows = pl.ds(i * tall, tall)
            half_way = jnp.dot(buf["lroot"][rows, :], grad, preferred_element_type=F32).astype(BF16)
            p = jnp.dot(half_way, buf["rroot"][...], preferred_element_type=F32)
            pre[rows, :] = p
            squares = squares + jnp.sum((p * p).reshape(tall // 8, 8, width), axis=0)
        gf = grad.astype(F32)
        grad_squares = jnp.sum((gf * gf).reshape(width // 8, 8, width), axis=0)
        count = width * width
        grad_mean = jnp.sum(grad_squares, axis=(0, 1), keepdims=True) / count
        pre_mean = jnp.sum(squares, axis=(0, 1), keepdims=True) / count
        factor = jnp.sqrt(grad_mean + epsilon) / jnp.sqrt(pre_mean + epsilon)
        for i in range(width // tall):
            rows = pl.ds(i * tall, tall)
            per = tall // strip
            shaped = (pre[rows, :] * factor).astype(BF16)
            buf["shaped"][pl.ds(i * per, per)] = shaped.reshape(per, strip, width)

        shaped, arrived = buf["shaped"], buf["arrived"]

        def give(o, _):
            to = peer(o)
            pltpu.make_async_remote_copy(
                src_ref=shaped.at[to], dst_ref=arrived.at[me], send_sem=a2a_send.at[n_rounds],
                recv_sem=a2a_recv.at[n_rounds], device_id=(to, ten), device_id_type=MESH,
            ).start()
            return 0

        local = (pre_mean / (pre_mean + epsilon)) * (grad_mean + epsilon) * count
        local = lax.select(mine, local, jnp.zeros_like(local))
        local = jnp.broadcast_to(local, (8, 128))

        def exchange(ref, n, dev, at, value):
            ref[0] = value
            if n == 1:
                return value
            for o in range(1, n):
                pltpu.make_async_remote_copy(
                    src_ref=ref.at[0], dst_ref=ref.at[o], send_sem=sum_send.at[at], recv_sem=sum_recv.at[at],
                    device_id=dev(o), device_id_type=MESH,
                ).start()

            def finish():
                part = ref.at[pl.ds(1, n - 1)]
                pltpu.make_async_copy(part, part, sum_recv.at[at]).wait()
                return jnp.sum(ref[...], axis=0)

            return finish

        finish = exchange(buf["sum_t"], n_tensor, lambda o: (me, lax.rem(ten + o, n_tensor)), 0, local)
        lax.fori_loop(1, n_dp, give, 0)
        arrived[me] = shaped[me]

        gram_weight = (1.0 - decay_rate) / width

        def statistic(factor_ref, gram):
            add = gram_weight * gram
            add = lax.select(mine, add, jnp.zeros_like(add))
            return decay_rate * factor_ref + add

        for i in range(width // tall):
            rows = pl.ds(i * tall, tall)
            gram = jnp.zeros((tall, width), F32)
            for k in range(n_rounds):
                gk = buf[f"grad_{k}"]
                per = tall // strip
                top = gk[pl.ds(i * per, per)].reshape(tall, ROUNDS[k][1])
                gram = gram + lax.dot_general(top, gk[...].reshape(width, ROUNDS[k][1]), (((1,), (1,)), ((), ())),
                                              preferred_element_type=F32)
            buf["lfac"][rows, :] = statistic(buf["lfac"][rows, :], gram)
        out_left = pltpu.make_async_copy(buf["lfac"], nl_ref, out_sem.at[0])
        out_left.start()
        if n_tensor > 1:
            local = finish()
        finish = exchange(buf["sum_y"], NY, lambda o: (z * NY + lax.rem(y + o, NY), ten), 1, local)
        flipped = grad.T
        for i in range(width // tall):
            rows = pl.ds(i * tall, tall)
            gram = jnp.dot(flipped[i * tall:(i + 1) * tall], grad, preferred_element_type=F32)
            buf["rfac"][rows, :] = statistic(buf["rfac"][rows, :], gram)
        out_right = pltpu.make_async_copy(buf["rfac"], nr_ref, out_sem.at[1])
        out_right.start()
        local = finish()
        finish = exchange(buf["sum_z"], nz, lambda o: (lax.rem(z + o, nz) * NY + y, ten), 2, local)
        local = finish()
        entries = nb_all * n_tensor * width * width
        scale = 1.0 / jnp.sqrt(local / entries + epsilon)
        scale = jnp.broadcast_to(scale[0:1, 0:1], (strip, width))
        a2a_all(a2a_recv.at[n_rounds], arrived).wait()
        for j in range(nb_all):
            dir_ref[j] = (arrived[owners_ref[0, j]].astype(F32) * scale).astype(BF16)

        for c in copies.values():
            c.wait_send()
        for k in range(n_rounds):
            a2a_all(a2a_send.at[k], buf[f"stage_{k}"]).wait()
        a2a_all(a2a_send.at[n_rounds], shaped).wait()
        for at, (n, ref) in enumerate(((n_tensor, buf["sum_t"]), (NY, buf["sum_y"]), (nz, buf["sum_z"]))):
            if n > 1:
                part = ref.at[pl.ds(1, n - 1)]
                pltpu.make_async_copy(part, part, sum_send.at[at]).wait()
        out_left.wait()
        out_right.wait()

    hbm = pl.BlockSpec(memory_space=pl.ANY)
    vmem = pl.BlockSpec(memory_space=pltpu.VMEM)
    new_left, new_right, directions = pl.pallas_call(
        kernel,
        out_shape=(
            jax.ShapeDtypeStruct((width, width), F32),
            jax.ShapeDtypeStruct((width, width), F32),
            jax.ShapeDtypeStruct((nb_all, strip, width), BF16),
        ),
        in_specs=[pl.BlockSpec(memory_space=pltpu.SMEM)] + [hbm] * 5,
        out_specs=(hbm, hbm, vmem),
        scratch_shapes=shapes
        + [
            pltpu.SemaphoreType.DMA((n_msg,)),
            pltpu.SemaphoreType.DMA((n_msg,)),
            pltpu.SemaphoreType.DMA((n_rounds,)),
            pltpu.SemaphoreType.DMA((4,)),
            pltpu.SemaphoreType.DMA((n_rounds + 1,)),
            pltpu.SemaphoreType.DMA((n_rounds + 1,)),
            pltpu.SemaphoreType.DMA((3,)),
            pltpu.SemaphoreType.DMA((3,)),
            pltpu.SemaphoreType.DMA((2,)),
        ],
        compiler_params=pltpu.CompilerParams(
            collective_id=0, has_side_effects=True, vmem_limit_bytes=48 * 1024 * 1024
        ),
        name="shampoo",
    )(owners, g, left_factor[0, 0], right_factor[0, 0], left_root[0, 0], right_root[0, 0])
    return new_left[None, None], new_right[None, None], directions


def solution(mesh):
    nz = mesh.shape["dp"] // NY
    return jax.shard_map(
        functools.partial(per_device, nz, mesh.shape["tensor"]),
        mesh=mesh,
        in_specs=(
            P("dp", "tensor", None, None),
            P("tensor", None),
            P("tensor", "dp", None, None),
            P("tensor", "dp", None, None),
            P("tensor", "dp", None, None),
            P("tensor", "dp", None, None),
        ),
        out_specs=(
            P("tensor", "dp", None, None),
            P("tensor", "dp", None, None),
            P("tensor", "dp", None),
        ),
        check_vma=False,
    )
```

time: 513 us -> 94.6 us (0.18)
  waiting for transfers between devices: 377 us -> 0 us
  Pallas kernels: 0 us -> 84.6 us
  blocking collectives: 75 us -> 0 us
  matrix products: 18.6 us -> 0 us
  between operations: 16.2 us -> 0.65 us
  local copies, waits for them, and re-layouts: 19.3 us -> 7.78 us
    reduce_scatter x1 -> x0, waiting for transfers between devices: 247 us -> none  [per_device(): lax.psum_scatter(jnp.einsum('sn,nab->sab', select, blocks, preferred_elem...]
    all_gather x1 -> x0, waiting for transfers between devices: 130 us -> none  [per_device(): gathered = lax.all_gather(scaled[None], 'dp', axis=0, tiled=True)]
    pallas_call x0 -> x1, Pallas kernels: none -> 84.6 us  [per_device(): pl.pallas_call(kernel, out_shape=(jax.ShapeDtypeStruct((width, width), F3...]
    psum x1 -> x0, blocking collectives: 75 us -> none  [per_device(): global_sum = lax.psum(local_sum, ('dp', 'tensor'))]
    dot_general x5 -> x0, matrix products: 18.6 us -> none  [the longest x1 9.91 us: per_device(): jnp.einsum('sn,nab->sab', select, blocks, preferred_element_type=jnp.floa...]
    convert_element_type x1 -> x0, local copies, waits for them, and re-layouts: 16.8 us -> none  [per_device(): jnp.einsum('sn,nab->sab', select, blocks, preferred_element_type=jnp.floa...]
    unnamed x7 -> x13, local copies, waits for them, and re-layouts: 0.72 us -> 7.78 us
  transfers between devices with their start and end apart: 2 -> 0, of which waited for: 2 -> 0; matrix products, arithmetic and copies ran while one was open for 1% -> 0% of each run, Pallas kernels for 0% -> 0%
where the time goes in v1:
time: 94.6 us; the launch traced here: 93 us
  Pallas kernels  84.6 us (89%)
  local copies, waits for them, and re-layouts  7.78 us (8%)
    pallas_call x1, Pallas kernels, per_device(): pl.pallas_call(kernel, out_shape=(jax.ShapeDtypeStruct((width, width), F3...  84.6 us
    unnamed x13, local copies, waits for them, and re-layouts  7.78 us

profile of v1, /device:TPU:32, one launch (start us, length us, event | category | flops | bytes accessed | tf_op | source)
XLA Modules:
  0.0 93.0 jit_solution(5454787395971322643)
XLA Ops:
  0.6 0.0 copy-start
  0.6 1.2 %copy-done = f32[1,1,512,512]{3,2,1,0:T(8,128)S(1)} copy-done((f32[1,1,512,512]{3,2,1,0:T(8,128)S(1)}, f32[1,1,512,512]{3,2,1,0:T(8,128)}, u32[]{:S(2)}) %copy-start) | copy-done | bytes 1048600
  1.9 0.0 copy-start.1
  1.9 1.2 %copy-done.1 = f32[1,1,512,512]{3,2,1,0:T(8,128)S(1)} copy-done((f32[1,1,512,512]{3,2,1,0:T(8,128)S(1)}, f32[1,1,512,512]{3,2,1,0:T(8,128)}, u32[]{:S(2)}) %copy-start.1) | copy-done | bytes 1048600
  3.1 0.0 copy-start.2
  3.1 1.0 %copy-done.2 = bf16[1,1,512,512]{3,2,1,0:T(8,128)(2,1)S(1)} copy-done((bf16[1,1,512,512]{3,2,1,0:T(8,128)(2,1)S(1)}, bf16[1,1,512,512]{3,2,1,0:T(8,128)(2,1)}, u32[]{:S(2)}) %copy-start.2) | copy-done | bytes 524312
  4.1 0.0 copy-start.3
  4.1 1.0 %copy-done.3 = bf16[1,1,512,512]{3,2,1,0:T(8,128)(2,1)S(1)} copy-done((bf16[1,1,512,512]{3,2,1,0:T(8,128)(2,1)S(1)}, bf16[1,1,512,512]{3,2,1,0:T(8,128)(2,1)}, u32[]{:S(2)}) %copy-start.3) | copy-done | bytes 524312
  5.2 0.0 copy-start.4
  5.2 0.7 copy-done.4
  5.8 84.6 %shampoo.1 = (f32[512,512]{1,0:T(8,128)S(1)}, f32[512,512]{1,0:T(8,128)S(1)}, bf16[8,16,512]{2,1,0:T(8,128)(2,1)S(1)}) custom-call(s32[1,32]{1,0:T(1,128)S(1)} %copy-done.4, bf16[8,8,4,16,512]{4,3,2,1,0:T(8,128)(2,1)} %bitcast.13, f32[512,512]{1,0:T(8,128)S(1)} %bitcast.9, f32[512,512]{1,0:T(8,128)S(1)} %bitcast.10, bf16[512,512]{1,0:T(8,128)(2,1)S(1)} %bitcast.11, ...), custom_call_target="tpu_custom_call" | custom-call | tf_op jit(solution)/shard_map/shampoo/pallas_call | solution.py:449
  90.4 1.0 %copy.12 = f32[1,1,512,512]{3,2,1,0:T(8,128)} copy(f32[1,1,512,512]{3,2,1,0:T(8,128)S(1)} %bitcast.8) | data formatting | bytes 2097152
  91.4 1.0 %copy.13 = f32[1,1,512,512]{3,2,1,0:T(8,128)} copy(f32[1,1,512,512]{3,2,1,0:T(8,128)S(1)} %bitcast.7) | data formatting | bytes 2097152
  92.4 0.7 copy.14
Async XLA Ops:
  0.6 1.2 %copy-start = (f32[1,1,512,512]{3,2,1,0:T(8,128)S(1)}, f32[1,1,512,512]{3,2,1,0:T(8,128)}, u32[]{:S(2)}) copy-start(f32[1,1,512,512]{3,2,1,0:T(8,128)} %param.8) | copy-start | bytes 3145732
  1.9 1.2 %copy-start.1 = (f32[1,1,512,512]{3,2,1,0:T(8,128)S(1)}, f32[1,1,512,512]{3,2,1,0:T(8,128)}, u32[]{:S(2)}) copy-start(f32[1,1,512,512]{3,2,1,0:T(8,128)} %param.9) | copy-start | bytes 3145732
  3.1 1.0 %copy-start.2 = (bf16[1,1,512,512]{3,2,1,0:T(8,128)(2,1)S(1)}, bf16[1,1,512,512]{3,2,1,0:T(8,128)(2,1)}, u32[]{:S(2)}) copy-start(bf16[1,1,512,512]{3,2,1,0:T(8,128)(2,1)} %param.10) | copy-start | bytes 1572868
  4.1 1.0 %copy-start.3 = (bf16[1,1,512,512]{3,2,1,0:T(8,128)(2,1)S(1)}, bf16[1,1,512,512]{3,2,1,0:T(8,128)(2,1)}, u32[]{:S(2)}) copy-start(bf16[1,1,512,512]{3,2,1,0:T(8,128)(2,1)} %param.11) | copy-start | bytes 1572868
  5.2 0.7 copy-start.4

commit v2 on v1

--- a/solution.py
+++ b/solution.py
@@ -15,21 +15,28 @@
 NY = 4
 
 ROUNDS = (
-    (0, 256, (3, 3, 1, 1)),
-    (256, 256, (3, 2, 1, 2)),
+    (0, 256, ((3, "y", 1, "cd"), (3, "y", -1, "cd"), (1, "z", 1, "cd"), (1, "z", -1, "cd"))),
+    (256, 256, ((2, "y", 1, "cd"), (2, "y", -1, "cd"), (2, "z", 1, "cd"), (2, "z", -1, "cd"))),
 )
-
-
-def sets_of(counts):
-    at, found = 0, []
-    for nb, (yfirst, s) in zip(counts, ((True, 1), (True, -1), (False, 1), (False, -1))):
-        if nb:
-            found.append((at, nb, yfirst, s))
-        at += nb
-    return found
-
-
-def plan(events, rate=0.18, latency=1.5, lead=2.0):
+FULL = False
+FOLD = 0.002
+YFAR = (1, -1, 2)
+ZFAR = (1, -1, 2, -2, 3, -3, 4)
+MODEL = (46.5, 2.2, 3.0)
+
+
+class Whole:
+    def __init__(self, ref, send, recv):
+        self.ref, self.send, self.recv = ref, send, recv
+
+    def wait_recv(self):
+        pltpu.make_async_copy(self.ref, self.ref, self.recv).wait()
+
+    def wait_send(self):
+        pltpu.make_async_copy(self.ref, self.ref, self.send).wait()
+
+
+def plan(events, rate, latency, lead):
     free = dict.fromkeys(("y1", "y-1", "z1", "z-1"), 0.0)
     arrive, done, order, now = {}, {}, [], 0.0
     left = list(events)
@@ -47,7 +54,7 @@
         (ready, _), e = best
         now = ready + e["cost"]
         for name, link, kib in e["sends"]:
-            free[link] = max(free[link], now) + kib * 1.024 / 100 * 2 / 0.9
+            free[link] = max(free[link], now) + kib * 1.024 / rate
             arrive[name] = free[link] + latency
         done[e["name"]] = now
         order.append(e)
@@ -60,7 +67,12 @@
     n_dp = nz * NY
     strip = width // n_dp
     g = gradients.reshape(nb_all, nz, NY, strip, width)
-    sets = [(k, c0, w) + s for k, (c0, w, counts) in enumerate(ROUNDS) for s in sets_of(counts)]
+    sets = []
+    for k, (c0, w, found) in enumerate(ROUNDS):
+        b0 = 0
+        for nb, axis, s, forms in found:
+            sets.append((k, c0, w, b0, nb, axis == "y", s, forms))
+            b0 += nb
     names, shapes = [], []
 
     def buffer(name, shape, dtype=BF16):
@@ -68,18 +80,29 @@
         shapes.append(pltpu.VMEM(shape, dtype))
 
     messages = {}
-    for i, (k, c0, w, b0, nb, yfirst, s) in enumerate(sets):
+    half = nz // 2
+    for i, (k, c0, w, b0, nb, yfirst, s, forms) in enumerate(sets):
         ychunk = (nb, nz, strip, w) if yfirst else (nb, strip, w)
         zchunk = (nb, strip, w) if yfirst else (nb, NY, strip, w)
-        for n in ("ry1", "ry2", "ry3", "sy"):
-            buffer(f"{n}_{i}", ychunk)
+        yform, zform = forms if yfirst else forms[::-1]
         buffer(f"mid_{i}", ychunk if yfirst else zchunk)
-        half = nz // 2
-        buffer(f"rza_{i}", (half,) + zchunk)
-        buffer(f"rzb_{i}", (half - 1,) + zchunk)
-        buffer(f"sza_{i}", (half - 1,) + zchunk)
-        buffer(f"szb_{i}", (half - 2,) + zchunk)
-        for n in ["y1", "y2", "y3"] + [f"a{h}" for h in range(half)] + [f"b{h}" for h in range(half - 1)]:
+        if yform == "c":
+            for n in ("ry1", "ry2", "ry3", "sy"):
+                buffer(f"{n}_{i}", ychunk)
+            found = ["y1", "y2", "y3"]
+        else:
+            buffer(f"ry_{i}", (NY - 1,) + ychunk)
+            found = ["y"]
+        if zform == "c":
+            buffer(f"rza_{i}", (half,) + zchunk)
+            buffer(f"rzb_{i}", (half - 1,) + zchunk)
+            buffer(f"sza_{i}", (half - 1,) + zchunk)
+            buffer(f"szb_{i}", (half - 2,) + zchunk)
+            found += [f"a{h}" for h in range(half)] + [f"b{h}" for h in range(half - 1)]
+        else:
+            buffer(f"rz_{i}", (nz - 1,) + zchunk)
+            found += ["z"]
+        for n in found:
             messages[f"{n}_{i}"] = len(messages)
     for k, (c0, w, _) in enumerate(ROUNDS):
         buffer(f"agg_{k}", (nb_all, strip, w))
@@ -91,6 +114,8 @@
     buffer("lfac", (width, width), F32)
     buffer("rfac", (width, width), F32)
     buffer("pre", (width, width), F32)
+    buffer("half", (width, width))
+    buffer("gsq", (len(ROUNDS), 8, 128), F32)
     buffer("shaped", (n_dp, strip, width))
     buffer("arrived", (n_dp, strip, width))
     buffer("sum_t", (n_tensor, 8, 128), F32)
@@ -102,7 +127,7 @@
 
     def kernel(owners_ref, g_ref, lf_ref, rf_ref, lr_ref, rr_ref, nl_ref, nr_ref, dir_ref, *scratch):
         buf = dict(zip(names, scratch))
-        send, recv, own_sem, load_sem, a2a_send, a2a_recv, sum_send, sum_recv, out_sem = scratch[len(names):]
+        send, recv, own_sem, load_sem, a2a_send, a2a_recv, sum_send, sum_recv = scratch[len(names):]
         me, ten = lax.axis_index("dp"), lax.axis_index("tensor")
         z, y = me // NY, me % NY
 
@@ -120,14 +145,15 @@
 
         barrier = pltpu.get_barrier_semaphore()
 
-        def greet(o, _):
-            pl.semaphore_signal(barrier, inc=1, device_id=(lax.rem(me + o, n_dp), ten), device_id_type=MESH)
-            return 0
-
-        lax.fori_loop(1, n_dp, greet, 0)
-        for o in range(1, n_tensor):
-            pl.semaphore_signal(barrier, inc=1, device_id=(me, lax.rem(ten + o, n_tensor)), device_id_type=MESH)
-        pl.semaphore_wait(barrier, n_dp - 1 + n_tensor - 1)
+        met = [ydev(d) for d in (1, -1, 2)] + [zdev(d) for d in (1, -1, 2, -2, 3, -3, 4)]
+        met += [(me, lax.rem(ten + o, n_tensor)) for o in range(1, n_tensor)]
+        if FULL:
+            met += [(zat(dz) * NY + yat(dy), ten) for dz in range(1, nz) for dy in range(1, NY)]
+
+        def greet():
+            for dev in met:
+                pl.semaphore_signal(barrier, inc=1, device_id=dev, device_id_type=MESH)
+            pl.semaphore_wait(barrier, len(met))
 
         own_copies = []
         for k, (c0, w, _) in enumerate(ROUNDS):
@@ -173,9 +199,9 @@
                 loaded.add(k)
                 own_copies[k].wait()
 
-        half = nz // 2
         finals = {k: [] for k in range(n_rounds)}
-        for i, (k, c0, w, b0, nb, yfirst, s) in enumerate(sets):
+        for i, (k, c0, w, b0, nb, yfirst, s, forms) in enumerate(sets):
+            yform, zform = forms if yfirst else forms[::-1]
             cols = pl.ds(c0, w)
             blocks = pl.ds(b0, nb)
             kib = nb * strip * w * 2 / 1024
@@ -208,8 +234,9 @@
             z_raw = own_z(mid if yfirst else g_ref)
             z_own = own_z(mid if yfirst else buf["own"])
             agg = buf[f"agg_{k}"].at[blocks]
-            ry1, ry2, ry3, sy = (buf[f"{n}_{i}"] for n in ("ry1", "ry2", "ry3", "sy"))
-            rza, rzb, sza, szb = (buf[f"{n}_{i}"] for n in ("rza", "rzb", "sza", "szb"))
+            ry1, ry2, ry3, sy = (buf.get(f"{n}_{i}") for n in ("ry1", "ry2", "ry3", "sy"))
+            rza, rzb, sza, szb = (buf.get(f"{n}_{i}") for n in ("rza", "rzb", "sza", "szb"))
+            ry, rz = buf.get(f"ry_{i}"), buf.get(f"rz_{i}")
             ylead = (yfirst, nz)
             zlead = (not yfirst, NY)
             up, down = s, -s
@@ -236,42 +263,80 @@
                 copies[f"y3_{i}"].wait_recv()
                 fold(dst, [ry2, ry3, y_own(0)], *ylead)
 
-            event(f"y0_{i}", y0, yk, after=ybase,
-                  sends=[(f"y1_{i}", yl[1], ysize), (f"y3_{i}", yl[-1], ysize)])
-            event(f"y1_{i}", y1, yk - 1, needs=[f"y1_{i}"], sends=[(f"y2_{i}", yl[1], ysize)])
-            event(f"ydone_{i}", y2, yk - 2, needs=[f"y2_{i}", f"y3_{i}"])
+            def straight(name, raw, into, far, dev):
+                i = messages[name]
+                for at, d in enumerate(far):
+                    pltpu.make_async_remote_copy(
+                        src_ref=raw(d), dst_ref=into.at[at], send_sem=send.at[i], recv_sem=recv.at[i],
+                        device_id=dev(d), device_id_type=MESH,
+                    ).start()
+                copies[name] = Whole(into, send.at[i], recv.at[i])
+
+            def ystart(i=i, y_raw=y_raw, ry=ry, straight=straight):
+                straight(f"y_{i}", y_raw, ry, YFAR, ydev)
+
+            def yend(i=i, k=k, y_own=y_own, ry=ry, fold=fold, ylead=ylead, dst=mid if yfirst else agg):
+                need_own(k)
+                copies[f"y_{i}"].wait_recv()
+                fold(dst, [y_own(0)] + [ry.at[at] for at in range(NY - 1)], *ylead)
+
+            def zflood(i=i, z_raw=z_raw, rz=rz, straight=straight):
+                straight(f"z_{i}", z_raw, rz, ZFAR, zdev)
+
+            def zsink(i=i, k=k, z_own=z_own, rz=rz, fold=fold, zlead=zlead, dst=agg if yfirst else mid):
+                need_own(k)
+                copies[f"z_{i}"].wait_recv()
+                fold(dst, [z_own(0)] + [rz.at[at] for at in range(nz - 1)], *zlead)
+
+            if yform == "c":
+                event(f"y0_{i}", y0, yk, after=ybase,
+                      sends=[(f"y1_{i}", yl[1], ysize), (f"y3_{i}", yl[-1], ysize)])
+                event(f"y1_{i}", y1, yk - 1, needs=[f"y1_{i}"], sends=[(f"y2_{i}", yl[1], ysize)], cost=0.1 + FOLD * ysize * 2)
+                event(f"ydone_{i}", y2, yk - 2, needs=[f"y2_{i}", f"y3_{i}"], cost=0.1 + FOLD * ysize * 3)
+            else:
+                event(f"y0_{i}", ystart, yk, after=ybase,
+                      sends=[(f"y+_{i}", yl[1], 2 * ysize), (f"y-_{i}", yl[-1], 2 * ysize)])
+                event(f"ydone_{i}", yend, yk - 2, needs=[f"y+_{i}", f"y-_{i}"], cost=0.1 + FOLD * ysize * 4)
+            if zform == "d":
+                event(f"z0_{i}", zflood, zk, after=zbase,
+                      sends=[(f"z+_{i}", zl[1], 8 * zsize), (f"z-_{i}", zl[-1], 8 * zsize)])
+                event(f"zdone_{i}", zsink, zk - 2, needs=[f"z+_{i}", f"z-_{i}"], cost=0.1 + FOLD * zsize * 8)
 
             def zstart(i=i, z_raw=z_raw, rza=rza, rzb=rzb, s=s):
                 put(f"a0_{i}", z_raw(half * s), rza.at[0], zdev(s))
                 put(f"b0_{i}", z_raw(-(half - 1) * s), rzb.at[0], zdev(-s))
 
-            event(f"z0_{i}", zstart, zk, after=zbase,
-                  sends=[(f"a0_{i}", zl[1], zsize), (f"b0_{i}", zl[-1], zsize)])
-            for h in range(1, half):
-                def za(i=i, k=k, h=h, z_own=z_own, rza=rza, sza=sza, s=s, fold=fold, zlead=zlead):
+            if zform == "c":
+                event(f"z0_{i}", zstart, zk, after=zbase,
+                      sends=[(f"a0_{i}", zl[1], zsize), (f"b0_{i}", zl[-1], zsize)])
+                for h in range(1, half):
+                    def za(i=i, k=k, h=h, z_own=z_own, rza=rza, sza=sza, s=s, fold=fold, zlead=zlead):
+                        need_own(k)
+                        copies[f"a{h - 1}_{i}"].wait_recv()
+                        fold(sza.at[h - 1], [rza.at[h - 1], z_own((half - h) * s)], *zlead)
+                        put(f"a{h}_{i}", sza.at[h - 1], rza.at[h], zdev(s))
+
+                    event(f"za{h}_{i}", za, zk - 1, needs=[f"a{h - 1}_{i}"], sends=[(f"a{h}_{i}", zl[1], zsize)],
+                          cost=0.1 + FOLD * zsize * 2)
+                for h in range(1, half - 1):
+                    def zb(i=i, k=k, h=h, z_own=z_own, rzb=rzb, szb=szb, s=s, fold=fold, zlead=zlead):
+                        need_own(k)
+                        copies[f"b{h - 1}_{i}"].wait_recv()
+                        fold(szb.at[h - 1], [rzb.at[h - 1], z_own(-(half - 1 - h) * s)], *zlead)
+                        put(f"b{h}_{i}", szb.at[h - 1], rzb.at[h], zdev(-s))
+
+                    event(f"zb{h}_{i}", zb, zk - 1, needs=[f"b{h - 1}_{i}"], sends=[(f"b{h}_{i}", zl[-1], zsize)],
+                          cost=0.1 + FOLD * zsize * 2)
+
+                def zend(i=i, k=k, z_own=z_own, rza=rza, rzb=rzb, fold=fold, zlead=zlead,
+                         dst=agg if yfirst else mid):
                     need_own(k)
-                    copies[f"a{h - 1}_{i}"].wait_recv()
-                    fold(sza.at[h - 1], [rza.at[h - 1], z_own((half - h) * s)], *zlead)
-                    put(f"a{h}_{i}", sza.at[h - 1], rza.at[h], zdev(s))
-
-                event(f"za{h}_{i}", za, zk - 1, needs=[f"a{h - 1}_{i}"], sends=[(f"a{h}_{i}", zl[1], zsize)])
-            for h in range(1, half - 1):
-                def zb(i=i, k=k, h=h, z_own=z_own, rzb=rzb, szb=szb, s=s, fold=fold, zlead=zlead):
-                    need_own(k)
-                    copies[f"b{h - 1}_{i}"].wait_recv()
-                    fold(szb.at[h - 1], [rzb.at[h - 1], z_own(-(half - 1 - h) * s)], *zlead)
-                    put(f"b{h}_{i}", szb.at[h - 1], rzb.at[h], zdev(-s))
-
-                event(f"zb{h}_{i}", zb, zk - 1, needs=[f"b{h - 1}_{i}"], sends=[(f"b{h}_{i}", zl[-1], zsize)])
-
-            def zend(i=i, k=k, z_own=z_own, rza=rza, rzb=rzb, fold=fold, zlead=zlead,
-                     dst=agg if yfirst else mid):
-                need_own(k)
-                copies[f"a{half - 1}_{i}"].wait_recv()
-                copies[f"b{half - 2}_{i}"].wait_recv()
-                fold(dst, [rza.at[half - 1], rzb.at[half - 2], z_own(0)], *zlead)
-
-            event(f"zdone_{i}", zend, zk - 2, needs=[f"a{half - 1}_{i}", f"b{half - 2}_{i}"])
+                    copies[f"a{half - 1}_{i}"].wait_recv()
+                    copies[f"b{half - 2}_{i}"].wait_recv()
+                    fold(dst, [rza.at[half - 1], rzb.at[half - 2], z_own(0)], *zlead)
+
+                event(f"zdone_{i}", zend, zk - 2, needs=[f"a{half - 1}_{i}", f"b{half - 2}_{i}"],
+                      cost=0.1 + FOLD * zsize * 3)
             finals[k].append(f"zdone_{i}" if yfirst else f"ydone_{i}")
 
         def block_of(device):
@@ -307,26 +372,42 @@
                   sends=[(f"rz{q}_{k}", f"z{q}", kib * 8 * NY) for q in (1, -1)]
                   + [(f"ry{q}_{k}", f"y{q}", kib * 2 * nz) for q in (1, -1)], cost=1.0)
 
+        def a2a_all(sem, ref):
+            part = ref.at[pl.ds(0, n_dp - 1)]
+            return pltpu.make_async_copy(part, part, sem)
+
+        waited = []
+
+        def land(k):
+            a2a_all(a2a_recv.at[k], buf[f"grad_{k}"]).wait()
+            if not waited:
+                waited.append(k)
+                for c in loads:
+                    c.wait()
+            w = ROUNDS[k][1]
+            gk = buf[f"grad_{k}"][...].reshape(width, w)
+            buf["half"][:, ROUNDS[k][0]:ROUNDS[k][0] + w] = jnp.dot(
+                buf["lroot"][...], gk, preferred_element_type=F32).astype(BF16)
+            gf = gk.astype(F32)
+            folded = jnp.sum((gf * gf).reshape(width // 8, 8, w), axis=0)
+            buf["gsq"][k] = sum(folded[:, c:c + 128] for c in range(0, w, 128))
+
+        for k in range(n_rounds):
+            event(f"land_{k}", functools.partial(land, k), k * 10 - 4,
+                  needs=[f"rz{q}_{k}" for q in (1, -1)] + [f"ry{q}_{k}" for q in (1, -1)], cost=0.7)
+
         for c in own_copies:
             c.start()
-        order, _ = plan(events)
-        n_first = 0
+        greet()
+        order, _ = plan(events, *MODEL)
         started = False
         for e in order:
-            if not started and e["needs"]:
+            if not started and (e["needs"] or e is order[-1]):
                 started = True
                 for c in loads:
                     c.start()
             e["emit"]()
 
-        def a2a_all(sem, ref):
-            part = ref.at[pl.ds(0, n_dp - 1)]
-            return pltpu.make_async_copy(part, part, sem)
-
-        for k in range(n_rounds):
-            a2a_all(a2a_recv.at[k], buf[f"grad_{k}"]).wait()
-        for c in loads:
-            c.wait()
 
         def whole():
             parts = [buf[f"grad_{k}"][...].reshape(width, ROUNDS[k][1]) for k in range(n_rounds)]
@@ -336,18 +417,15 @@
         for j in range(nb_all):
             owned = owned + jnp.where(owners_ref[0, j] == me, 1, 0)
         mine = owned > 0
-        grad = whole()
         tall = 128
         pre = buf["pre"]
         squares = jnp.zeros((8, width), F32)
         for i in range(width // tall):
             rows = pl.ds(i * tall, tall)
-            half_way = jnp.dot(buf["lroot"][rows, :], grad, preferred_element_type=F32).astype(BF16)
-            p = jnp.dot(half_way, buf["rroot"][...], preferred_element_type=F32)
+            p = jnp.dot(buf["half"][rows, :], buf["rroot"][...], preferred_element_type=F32)
             pre[rows, :] = p
             squares = squares + jnp.sum((p * p).reshape(tall // 8, 8, width), axis=0)
-        gf = grad.astype(F32)
-        grad_squares = jnp.sum((gf * gf).reshape(width // 8, 8, width), axis=0)
+        grad_squares = jnp.sum(buf["gsq"][...], axis=0)
         count = width * width
         grad_mean = jnp.sum(grad_squares, axis=(0, 1), keepdims=True) / count
         pre_mean = jnp.sum(squares, axis=(0, 1), keepdims=True) / count
@@ -409,19 +487,16 @@
                 top = gk[pl.ds(i * per, per)].reshape(tall, ROUNDS[k][1])
                 gram = gram + lax.dot_general(top, gk[...].reshape(width, ROUNDS[k][1]), (((1,), (1,)), ((), ())),
                                               preferred_element_type=F32)
-            buf["lfac"][rows, :] = statistic(buf["lfac"][rows, :], gram)
-        out_left = pltpu.make_async_copy(buf["lfac"], nl_ref, out_sem.at[0])
-        out_left.start()
+            nl_ref[rows, :] = statistic(buf["lfac"][rows, :], gram)
         if n_tensor > 1:
             local = finish()
         finish = exchange(buf["sum_y"], NY, lambda o: (z * NY + lax.rem(y + o, NY), ten), 1, local)
+        grad = whole()
         flipped = grad.T
         for i in range(width // tall):
             rows = pl.ds(i * tall, tall)
             gram = jnp.dot(flipped[i * tall:(i + 1) * tall], grad, preferred_element_type=F32)
-            buf["rfac"][rows, :] = statistic(buf["rfac"][rows, :], gram)
-        out_right = pltpu.make_async_copy(buf["rfac"], nr_ref, out_sem.at[1])
-        out_right.start()
+            nr_ref[rows, :] = statistic(buf["rfac"][rows, :], gram)
         local = finish()
         finish = exchange(buf["sum_z"], nz, lambda o: (lax.rem(z + o, nz) * NY + y, ten), 2, local)
         local = finish()
@@ -441,20 +516,18 @@
             if n > 1:
                 part = ref.at[pl.ds(1, n - 1)]
                 pltpu.make_async_copy(part, part, sum_send.at[at]).wait()
-        out_left.wait()
-        out_right.wait()
 
     hbm = pl.BlockSpec(memory_space=pl.ANY)
     vmem = pl.BlockSpec(memory_space=pltpu.VMEM)
     new_left, new_right, directions = pl.pallas_call(
         kernel,
         out_shape=(
-            jax.ShapeDtypeStruct((width, width), F32),
-            jax.ShapeDtypeStruct((width, width), F32),
-            jax.ShapeDtypeStruct((nb_all, strip, width), BF16),
+            pltpu.VMEM((width, width), F32),
+            pltpu.VMEM((width, width), F32),
+            pltpu.VMEM((nb_all, strip, width), BF16),
         ),
         in_specs=[pl.BlockSpec(memory_space=pltpu.SMEM)] + [hbm] * 5,
-        out_specs=(hbm, hbm, vmem),
+        out_specs=(vmem, vmem, vmem),
         scratch_shapes=shapes
         + [
             pltpu.SemaphoreType.DMA((n_msg,)),
@@ -465,10 +538,9 @@
             pltpu.SemaphoreType.DMA((n_rounds + 1,)),
             pltpu.SemaphoreType.DMA((3,)),
             pltpu.SemaphoreType.DMA((3,)),
-            pltpu.SemaphoreType.DMA((2,)),
         ],
         compiler_params=pltpu.CompilerParams(
-            collective_id=0, has_side_effects=True, vmem_limit_bytes=48 * 1024 * 1024
+            collective_id=0, has_side_effects=True, vmem_limit_bytes=58 * 1024 * 1024
         ),
         name="shampoo",
     )(owners, g, left_factor[0, 0], right_factor[0, 0], left_root[0, 0], right_root[0, 0])

time: 94.6 us -> 75 us (0.79); the launches traced: 93 us -> 74.8 us
  Pallas kernels: 84.6 us -> 71.5 us
  local copies, waits for them, and re-layouts: 7.78 us -> 2.6 us
    pallas_call x1, Pallas kernels: 84.6 us -> 71.5 us  [per_device(): pl.pallas_call(kernel, out_shape=(pltpu.VMEM((width, width), F32), pltpu....]
    unnamed x13 -> x3, local copies, waits for them, and re-layouts: 7.78 us -> 2.6 us
where the time goes in v2:
time: 75 us; the launch traced here: 74.8 us
  Pallas kernels  71.5 us (95%)
  local copies, waits for them, and re-layouts  2.6 us (3%)
    pallas_call x1, Pallas kernels, per_device(): pl.pallas_call(kernel, out_shape=(pltpu.VMEM((width, width), F32), pltpu....  71.5 us
    unnamed x3, local copies, waits for them, and re-layouts  2.6 us

profile of v2, /device:TPU:32, one launch (start us, length us, event | category | flops | bytes accessed | tf_op | source)
XLA Modules:
  0.0 74.8 jit_solution(13382831446338257890)
XLA Ops:
  0.6 71.5 %shampoo.1 = (f32[512,512]{1,0:T(8,128)S(1)}, f32[512,512]{1,0:T(8,128)S(1)}, bf16[8,16,512]{2,1,0:T(8,128)(2,1)S(1)}) custom-call(s32[1,32]{1,0:T(1,128)} %owners_ref.1, bf16[8,8,4,16,512]{4,3,2,1,0:T(8,128)(2,1)} %bitcast.9, f32[512,512]{1,0:T(8,128)} %bitcast.10, f32[512,512]{1,0:T(8,128)} %bitcast.11, bf16[512,512]{1,0:T(8,128)(2,1)} %bitcast.12, ...), custom_call_target="tpu_custom_call" | custom-call | tf_op jit(solution)/shard_map/shampoo/pallas_call | solution.py:522
  72.2 1.0 %copy.12 = f32[1,1,512,512]{3,2,1,0:T(8,128)} copy(f32[1,1,512,512]{3,2,1,0:T(8,128)S(1)} %bitcast.8) | data formatting | bytes 2097152
  73.1 1.0 %copy.13 = f32[1,1,512,512]{3,2,1,0:T(8,128)} copy(f32[1,1,512,512]{3,2,1,0:T(8,128)S(1)} %bitcast.7) | data formatting | bytes 2097152
  74.1 0.7 copy.14

commit v3 on v2

--- a/solution.py
+++ b/solution.py
@@ -15,10 +15,27 @@
 NY = 4
 
 ROUNDS = (
-    (0, 256, ((3, "y", 1, "cd"), (3, "y", -1, "cd"), (1, "z", 1, "cd"), (1, "z", -1, "cd"))),
-    (256, 256, ((2, "y", 1, "cd"), (2, "y", -1, "cd"), (2, "z", 1, "cd"), (2, "z", -1, "cd"))),
+    (0, 128, (
+        (4, "y", 1, "ct", 13.1),
+        (3, "y", -1, "cc", 6.5),
+        (1, "z", 1, "cd", 7.2),
+    )),
+    (128, 256, (
+        (2, "y", -1, "ct", 15.8),
+        (3, "z", 1, "cd", 12.0),
+        (2, "z", -1, "cd", 21.6),
+        (1, "y", 1, "cd", 16.8),
+    )),
+    (384, 128, (
+        (4, "y", -1, "cd", 29.3),
+        (3, "z", 1, "cd", 19.8),
+        (1, "y", 1, "cd", 21.2),
+    )),
 )
 FULL = False
+GIVE = "near"
+FIRST = ((4, 12), (20, 28))
+LAST = ((1, 4), (12, 20), (28, 32))
 FOLD = 0.002
 YFAR = (1, -1, 2)
 ZFAR = (1, -1, 2, -2, 3, -3, 4)
@@ -70,8 +87,8 @@
     sets = []
     for k, (c0, w, found) in enumerate(ROUNDS):
         b0 = 0
-        for nb, axis, s, forms in found:
-            sets.append((k, c0, w, b0, nb, axis == "y", s, forms))
+        for nb, axis, s, forms, rank in found:
+            sets.append((k, c0, w, b0, nb, axis == "y", s, (forms, rank)))
             b0 += nb
     names, shapes = [], []
 
@@ -84,6 +101,7 @@
     for i, (k, c0, w, b0, nb, yfirst, s, forms) in enumerate(sets):
         ychunk = (nb, nz, strip, w) if yfirst else (nb, strip, w)
         zchunk = (nb, strip, w) if yfirst else (nb, NY, strip, w)
+        forms = forms[0]
         yform, zform = forms if yfirst else forms[::-1]
         buffer(f"mid_{i}", ychunk if yfirst else zchunk)
         if yform == "c":
@@ -99,6 +117,10 @@
             buffer(f"sza_{i}", (half - 1,) + zchunk)
             buffer(f"szb_{i}", (half - 2,) + zchunk)
             found += [f"a{h}" for h in range(half)] + [f"b{h}" for h in range(half - 1)]
+        elif zform == "t":
+            buffer(f"rt_{i}", (7,) + zchunk)
+            buffer(f"st_{i}", (2,) + zchunk)
+            found += [f"t{h}" for h in range(7)]
         else:
             buffer(f"rz_{i}", (nz - 1,) + zchunk)
             found += ["z"]
@@ -113,10 +135,9 @@
     buffer("rroot", (width, width))
     buffer("lfac", (width, width), F32)
     buffer("rfac", (width, width), F32)
-    buffer("pre", (width, width), F32)
+    buffer("pre", (n_dp, strip, width))
     buffer("half", (width, width))
     buffer("gsq", (len(ROUNDS), 8, 128), F32)
-    buffer("shaped", (n_dp, strip, width))
     buffer("arrived", (n_dp, strip, width))
     buffer("sum_t", (n_tensor, 8, 128), F32)
     buffer("sum_y", (NY, 8, 128), F32)
@@ -201,6 +222,7 @@
 
         finals = {k: [] for k in range(n_rounds)}
         for i, (k, c0, w, b0, nb, yfirst, s, forms) in enumerate(sets):
+            forms, rank = forms
             yform, zform = forms if yfirst else forms[::-1]
             cols = pl.ds(c0, w)
             blocks = pl.ds(b0, nb)
@@ -237,12 +259,13 @@
             ry1, ry2, ry3, sy = (buf.get(f"{n}_{i}") for n in ("ry1", "ry2", "ry3", "sy"))
             rza, rzb, sza, szb = (buf.get(f"{n}_{i}") for n in ("rza", "rzb", "sza", "szb"))
             ry, rz = buf.get(f"ry_{i}"), buf.get(f"rz_{i}")
+            rt, st = buf.get(f"rt_{i}"), buf.get(f"st_{i}")
             ylead = (yfirst, nz)
             zlead = (not yfirst, NY)
             up, down = s, -s
             yl, zl = {1: f"y{s}", -1: f"y{-s}"}, {1: f"z{s}", -1: f"z{-s}"}
-            yk = k * 10 + (0 if yfirst else 5)
-            zk = k * 10 + (5 if yfirst else 0)
+            yk, zk = (rank, k * 10 + 5) if yfirst else (k * 10 + 5, rank)
+            yr, zr = (k * 10, zk) if yfirst else (yk, k * 10)
             ybase = () if yfirst else (f"zdone_{i}",)
             zbase = (f"ydone_{i}",) if yfirst else ()
 
@@ -288,19 +311,46 @@
                 copies[f"z_{i}"].wait_recv()
                 fold(dst, [z_own(0)] + [rz.at[at] for at in range(nz - 1)], *zlead)
 
+            def zpairs(i=i, z_raw=z_raw, rt=rt, s=s):
+                for at, (chunk, to) in enumerate(((4, 2), (3, 1), (-3, -1), (1, 1), (-1, -1))):
+                    put(f"t{at}_{i}", z_raw(chunk * s), rt.at[at], zdev(to * s))
+
+            def zjoin(i=i, k=k, z_own=z_own, rt=rt, st=st, s=s, fold=fold, zlead=zlead):
+                need_own(k)
+                for at in range(3):
+                    copies[f"t{at}_{i}"].wait_recv()
+                fold(st.at[0], [rt.at[0], rt.at[1], z_own(2 * s)], *zlead)
+                put(f"t5_{i}", st.at[0], rt.at[5], zdev(2 * s))
+                fold(st.at[1], [rt.at[2], z_own(-2 * s)], *zlead)
+                put(f"t6_{i}", st.at[1], rt.at[6], zdev(-2 * s))
+
+            def zmeet(i=i, k=k, z_own=z_own, rt=rt, fold=fold, zlead=zlead, dst=agg if yfirst else mid):
+                need_own(k)
+                for at in range(3, 7):
+                    copies[f"t{at}_{i}"].wait_recv()
+                fold(dst, [z_own(0)] + [rt.at[at] for at in range(3, 7)], *zlead)
+
             if yform == "c":
                 event(f"y0_{i}", y0, yk, after=ybase,
                       sends=[(f"y1_{i}", yl[1], ysize), (f"y3_{i}", yl[-1], ysize)])
-                event(f"y1_{i}", y1, yk - 1, needs=[f"y1_{i}"], sends=[(f"y2_{i}", yl[1], ysize)], cost=0.1 + FOLD * ysize * 2)
-                event(f"ydone_{i}", y2, yk - 2, needs=[f"y2_{i}", f"y3_{i}"], cost=0.1 + FOLD * ysize * 3)
+                event(f"y1_{i}", y1, yr - 1, needs=[f"y1_{i}"], sends=[(f"y2_{i}", yl[1], ysize)], cost=0.1 + FOLD * ysize * 2)
+                event(f"ydone_{i}", y2, yr - 2, needs=[f"y2_{i}", f"y3_{i}"], cost=0.1 + FOLD * ysize * 3)
             else:
                 event(f"y0_{i}", ystart, yk, after=ybase,
                       sends=[(f"y+_{i}", yl[1], 2 * ysize), (f"y-_{i}", yl[-1], 2 * ysize)])
-                event(f"ydone_{i}", yend, yk - 2, needs=[f"y+_{i}", f"y-_{i}"], cost=0.1 + FOLD * ysize * 4)
+                event(f"ydone_{i}", yend, yr - 2, needs=[f"y+_{i}", f"y-_{i}"], cost=0.1 + FOLD * ysize * 4)
+            if zform == "t":
+                event(f"z0_{i}", zpairs, zk, after=zbase,
+                      sends=[(f"t+_{i}", zl[1], 3 * zsize), (f"t-_{i}", zl[-1], zsize),
+                             (f"T+_{i}", zl[1], zsize), (f"T-_{i}", zl[-1], zsize)])
+                event(f"z1_{i}", zjoin, zr - 1, needs=[f"t+_{i}", f"t-_{i}"],
+                      sends=[(f"u+_{i}", zl[1], 2 * zsize), (f"u-_{i}", zl[-1], 2 * zsize)], cost=0.2 + FOLD * zsize * 5)
+                event(f"zdone_{i}", zmeet, zr - 2, needs=[f"u+_{i}", f"u-_{i}", f"T+_{i}", f"T-_{i}"],
+                      cost=0.1 + FOLD * zsize * 5)
             if zform == "d":
                 event(f"z0_{i}", zflood, zk, after=zbase,
                       sends=[(f"z+_{i}", zl[1], 8 * zsize), (f"z-_{i}", zl[-1], 8 * zsize)])
-                event(f"zdone_{i}", zsink, zk - 2, needs=[f"z+_{i}", f"z-_{i}"], cost=0.1 + FOLD * zsize * 8)
+                event(f"zdone_{i}", zsink, zr - 2, needs=[f"z+_{i}", f"z-_{i}"], cost=0.1 + FOLD * zsize * 8)
 
             def zstart(i=i, z_raw=z_raw, rza=rza, rzb=rzb, s=s):
                 put(f"a0_{i}", z_raw(half * s), rza.at[0], zdev(s))
@@ -316,7 +366,7 @@
                         fold(sza.at[h - 1], [rza.at[h - 1], z_own((half - h) * s)], *zlead)
                         put(f"a{h}_{i}", sza.at[h - 1], rza.at[h], zdev(s))
 
-                    event(f"za{h}_{i}", za, zk - 1, needs=[f"a{h - 1}_{i}"], sends=[(f"a{h}_{i}", zl[1], zsize)],
+                    event(f"za{h}_{i}", za, zr - 1, needs=[f"a{h - 1}_{i}"], sends=[(f"a{h}_{i}", zl[1], zsize)],
                           cost=0.1 + FOLD * zsize * 2)
                 for h in range(1, half - 1):
                     def zb(i=i, k=k, h=h, z_own=z_own, rzb=rzb, szb=szb, s=s, fold=fold, zlead=zlead):
@@ -325,7 +375,7 @@
                         fold(szb.at[h - 1], [rzb.at[h - 1], z_own(-(half - 1 - h) * s)], *zlead)
                         put(f"b{h}_{i}", szb.at[h - 1], rzb.at[h], zdev(-s))
 
-                    event(f"zb{h}_{i}", zb, zk - 1, needs=[f"b{h - 1}_{i}"], sends=[(f"b{h}_{i}", zl[-1], zsize)],
+                    event(f"zb{h}_{i}", zb, zr - 1, needs=[f"b{h - 1}_{i}"], sends=[(f"b{h}_{i}", zl[-1], zsize)],
                           cost=0.1 + FOLD * zsize * 2)
 
                 def zend(i=i, k=k, z_own=z_own, rza=rza, rzb=rzb, fold=fold, zlead=zlead,
@@ -335,7 +385,7 @@
                     copies[f"b{half - 2}_{i}"].wait_recv()
                     fold(dst, [rza.at[half - 1], rzb.at[half - 2], z_own(0)], *zlead)
 
-                event(f"zdone_{i}", zend, zk - 2, needs=[f"a{half - 1}_{i}", f"b{half - 2}_{i}"],
+                event(f"zdone_{i}", zend, zr - 2, needs=[f"a{half - 1}_{i}", f"b{half - 2}_{i}"],
                       cost=0.1 + FOLD * zsize * 3)
             finals[k].append(f"zdone_{i}" if yfirst else f"ydone_{i}")
 
@@ -370,7 +420,7 @@
 
             event(f"route_{k}", route, k * 10 - 3, after=finals[k],
                   sends=[(f"rz{q}_{k}", f"z{q}", kib * 8 * NY) for q in (1, -1)]
-                  + [(f"ry{q}_{k}", f"y{q}", kib * 2 * nz) for q in (1, -1)], cost=1.0)
+                  + [(f"ry{q}_{k}", f"y{q}", kib * 2 * nz) for q in (1, -1)], cost=1.7)
 
         def a2a_all(sem, ref):
             part = ref.at[pl.ds(0, n_dp - 1)]
@@ -418,42 +468,57 @@
             owned = owned + jnp.where(owners_ref[0, j] == me, 1, 0)
         mine = owned > 0
         tall = 128
-        pre = buf["pre"]
+        per = tall // strip
+        pre, arrived = buf["pre"], buf["arrived"]
+
+        def give(to):
+            pltpu.make_async_remote_copy(
+                src_ref=pre.at[to], dst_ref=arrived.at[me], send_sem=a2a_send.at[n_rounds],
+                recv_sem=a2a_recv.at[n_rounds], device_id=(to, ten), device_id_type=MESH,
+            ).start()
+
         squares = jnp.zeros((8, width), F32)
         for i in range(width // tall):
             rows = pl.ds(i * tall, tall)
             p = jnp.dot(buf["half"][rows, :], buf["rroot"][...], preferred_element_type=F32)
-            pre[rows, :] = p
+            pre[pl.ds(i * per, per)] = p.astype(BF16).reshape(per, strip, width)
             squares = squares + jnp.sum((p * p).reshape(tall // 8, 8, width), axis=0)
+            if GIVE == "early":
+                def some(o, _, i=i):
+                    to = i * per + lax.rem(me + o, per)
+
+                    @pl.when(to != me)
+                    def _():
+                        give(to)
+
+                    return 0
+
+                lax.fori_loop(0, per, some, 0)
+        def give_to(spans):
+            for first, last in spans:
+                lax.fori_loop(first, last, lambda o, _: (give(peer(o)), 0)[1], 0)
+
+        if GIVE == "split":
+            give_to(FIRST)
+        arrived[me] = pre[me]
+
         grad_squares = jnp.sum(buf["gsq"][...], axis=0)
         count = width * width
         grad_mean = jnp.sum(grad_squares, axis=(0, 1), keepdims=True) / count
         pre_mean = jnp.sum(squares, axis=(0, 1), keepdims=True) / count
         factor = jnp.sqrt(grad_mean + epsilon) / jnp.sqrt(pre_mean + epsilon)
-        for i in range(width // tall):
-            rows = pl.ds(i * tall, tall)
-            per = tall // strip
-            shaped = (pre[rows, :] * factor).astype(BF16)
-            buf["shaped"][pl.ds(i * per, per)] = shaped.reshape(per, strip, width)
-
-        shaped, arrived = buf["shaped"], buf["arrived"]
-
-        def give(o, _):
-            to = peer(o)
-            pltpu.make_async_remote_copy(
-                src_ref=shaped.at[to], dst_ref=arrived.at[me], send_sem=a2a_send.at[n_rounds],
-                recv_sem=a2a_recv.at[n_rounds], device_id=(to, ten), device_id_type=MESH,
-            ).start()
-            return 0
-
-        local = (pre_mean / (pre_mean + epsilon)) * (grad_mean + epsilon) * count
-        local = lax.select(mine, local, jnp.zeros_like(local))
-        local = jnp.broadcast_to(local, (8, 128))
+        share = (pre_mean / (pre_mean + epsilon)) * (grad_mean + epsilon) * count
+        owned, block = jnp.int32(0), jnp.int32(0)
+        for j in range(nb_all):
+            here = owners_ref[0, j] == me
+            owned = owned + jnp.where(here, 1, 0)
+            block = jnp.where(here, j, block)
+        mine = owned > 0
+        share = lax.select(mine, share, jnp.zeros_like(share))
+        factor = lax.select(mine, factor, jnp.zeros_like(factor))
 
         def exchange(ref, n, dev, at, value):
             ref[0] = value
-            if n == 1:
-                return value
             for o in range(1, n):
                 pltpu.make_async_remote_copy(
                     src_ref=ref.at[0], dst_ref=ref.at[o], send_sem=sum_send.at[at], recv_sem=sum_recv.at[at],
@@ -461,15 +526,27 @@
                 ).start()
 
             def finish():
-                part = ref.at[pl.ds(1, n - 1)]
-                pltpu.make_async_copy(part, part, sum_recv.at[at]).wait()
+                if n > 1:
+                    part = ref.at[pl.ds(1, n - 1)]
+                    pltpu.make_async_copy(part, part, sum_recv.at[at]).wait()
                 return jnp.sum(ref[...], axis=0)
 
             return finish
 
-        finish = exchange(buf["sum_t"], n_tensor, lambda o: (me, lax.rem(ten + o, n_tensor)), 0, local)
-        lax.fori_loop(1, n_dp, give, 0)
-        arrived[me] = shaped[me]
+        finish = exchange(buf["sum_t"], n_tensor, lambda o: (me, lax.rem(ten + o, n_tensor)), 0,
+                          jnp.broadcast_to(share, (8, 128)))
+        if GIVE == "near":
+            lax.fori_loop(1, n_dp, lambda o, _: (give(peer(o)), 0)[1], 0)
+        if GIVE == "far":
+            lax.fori_loop(1, n_dp, lambda o, _: (give(peer(n_dp - o)), 0)[1], 0)
+
+        lanes = lax.broadcasted_iota(jnp.int32, (8, 128), 1)
+        in_row = lax.broadcasted_iota(jnp.int32, (8, 128), 0) == block
+        local = jnp.where(lanes < 64, jnp.where(in_row, jnp.broadcast_to(factor, (8, 128)), 0.0), finish())
+        finish = exchange(buf["sum_y"], NY, lambda o: (z * NY + lax.rem(y + o, NY), ten), 1, local)
+        finish = exchange(buf["sum_z"], nz, lambda o: (lax.rem(z + o, nz) * NY + y, ten), 2, finish())
+        if GIVE == "split":
+            give_to(LAST)
 
         gram_weight = (1.0 - decay_rate) / width
 
@@ -488,34 +565,30 @@
                 gram = gram + lax.dot_general(top, gk[...].reshape(width, ROUNDS[k][1]), (((1,), (1,)), ((), ())),
                                               preferred_element_type=F32)
             nl_ref[rows, :] = statistic(buf["lfac"][rows, :], gram)
-        if n_tensor > 1:
-            local = finish()
-        finish = exchange(buf["sum_y"], NY, lambda o: (z * NY + lax.rem(y + o, NY), ten), 1, local)
         grad = whole()
         flipped = grad.T
         for i in range(width // tall):
             rows = pl.ds(i * tall, tall)
             gram = jnp.dot(flipped[i * tall:(i + 1) * tall], grad, preferred_element_type=F32)
             nr_ref[rows, :] = statistic(buf["rfac"][rows, :], gram)
-        local = finish()
-        finish = exchange(buf["sum_z"], nz, lambda o: (lax.rem(z + o, nz) * NY + y, ten), 2, local)
-        local = finish()
-        entries = nb_all * n_tensor * width * width
-        scale = 1.0 / jnp.sqrt(local / entries + epsilon)
-        scale = jnp.broadcast_to(scale[0:1, 0:1], (strip, width))
-        a2a_all(a2a_recv.at[n_rounds], arrived).wait()
-        for j in range(nb_all):
-            dir_ref[j] = (arrived[owners_ref[0, j]].astype(F32) * scale).astype(BF16)
-
         for c in copies.values():
             c.wait_send()
         for k in range(n_rounds):
             a2a_all(a2a_send.at[k], buf[f"stage_{k}"]).wait()
-        a2a_all(a2a_send.at[n_rounds], shaped).wait()
+
+        entries = nb_all * n_tensor * width * width
+        norms = finish()
+        scale = 1.0 / jnp.sqrt(norms[0:1, 64:65] / entries + epsilon)
         for at, (n, ref) in enumerate(((n_tensor, buf["sum_t"]), (NY, buf["sum_y"]), (nz, buf["sum_z"]))):
             if n > 1:
                 part = ref.at[pl.ds(1, n - 1)]
                 pltpu.make_async_copy(part, part, sum_send.at[at]).wait()
+        scale = jnp.broadcast_to(scale, (strip, width))
+        a2a_all(a2a_recv.at[n_rounds], arrived).wait()
+        for j in range(nb_all):
+            shaped = arrived[owners_ref[0, j]].astype(F32) * jnp.broadcast_to(norms[j:j + 1, 0:1], (strip, width))
+            dir_ref[j] = (shaped * scale).astype(BF16)
+        a2a_all(a2a_send.at[n_rounds], pre).wait()
 
     hbm = pl.BlockSpec(memory_space=pl.ANY)
     vmem = pl.BlockSpec(memory_space=pltpu.VMEM)

time: 75 us -> 72.3 us (0.964)
  Pallas kernels: 71.5 us -> 68.5 us
    pallas_call x1, Pallas kernels: 71.5 us -> 68.5 us  [per_device(): pl.pallas_call(kernel, out_shape=(pltpu.VMEM((width, width), F32), pltpu....]
where the time goes in v3:
time: 72.3 us; the launch traced here: 71.7 us
  Pallas kernels  68.5 us (95%)
  local copies, waits for them, and re-layouts  2.6 us (4%)
    pallas_call x1, Pallas kernels, per_device(): pl.pallas_call(kernel, out_shape=(pltpu.VMEM((width, width), F32), pltpu....  68.5 us
    unnamed x3, local copies, waits for them, and re-layouts  2.6 us

profile of v3, /device:TPU:32, one launch (start us, length us, event | category | flops | bytes accessed | tf_op | source)
XLA Modules:
  0.0 71.7 jit_solution(17039445688104847774)
XLA Ops:
  0.6 68.5 %shampoo.1 = (f32[512,512]{1,0:T(8,128)S(1)}, f32[512,512]{1,0:T(8,128)S(1)}, bf16[8,16,512]{2,1,0:T(8,128)(2,1)S(1)}) custom-call(s32[1,32]{1,0:T(1,128)} %owners_ref.1, bf16[8,8,4,16,512]{4,3,2,1,0:T(8,128)(2,1)} %bitcast.9, f32[512,512]{1,0:T(8,128)} %bitcast.10, f32[512,512]{1,0:T(8,128)} %bitcast.11, bf16[512,512]{1,0:T(8,128)(2,1)} %bitcast.12, ...), custom_call_target="tpu_custom_call" | custom-call | tf_op jit(solution)/shard_map/shampoo/pallas_call | solution.py:595
  69.1 1.0 %copy.12 = f32[1,1,512,512]{3,2,1,0:T(8,128)} copy(f32[1,1,512,512]{3,2,1,0:T(8,128)S(1)} %bitcast.8) | data formatting | bytes 2097152
  70.1 1.0 %copy.13 = f32[1,1,512,512]{3,2,1,0:T(8,128)} copy(f32[1,1,512,512]{3,2,1,0:T(8,128)S(1)} %bitcast.7) | data formatting | bytes 2097152
  71.0 0.7 copy.14

commit v4 on v3

--- a/solution.py
+++ b/solution.py
@@ -33,9 +33,6 @@
     )),
 )
 FULL = False
-GIVE = "near"
-FIRST = ((4, 12), (20, 28))
-LAST = ((1, 4), (12, 20), (28, 32))
 FOLD = 0.002
 YFAR = (1, -1, 2)
 ZFAR = (1, -1, 2, -2, 3, -3, 4)
@@ -54,7 +51,7 @@
 
 
 def plan(events, rate, latency, lead):
-    free = dict.fromkeys(("y1", "y-1", "z1", "z-1"), 0.0)
+    free = dict.fromkeys([(a, q) for a in "yz" for q in (1, -1)], 0.0)
     arrive, done, order, now = {}, {}, [], 0.0
     left = list(events)
     while left:
@@ -103,33 +100,33 @@
         zchunk = (nb, strip, w) if yfirst else (nb, NY, strip, w)
         forms = forms[0]
         yform, zform = forms if yfirst else forms[::-1]
-        buffer(f"mid_{i}", ychunk if yfirst else zchunk)
+        buffer(("mid", i), ychunk if yfirst else zchunk)
         if yform == "c":
             for n in ("ry1", "ry2", "ry3", "sy"):
-                buffer(f"{n}_{i}", ychunk)
-            found = ["y1", "y2", "y3"]
+                buffer((n, i), ychunk)
+            found = [("y1",), ("y2",), ("y3",)]
         else:
-            buffer(f"ry_{i}", (NY - 1,) + ychunk)
-            found = ["y"]
+            buffer(("ry", i), (NY - 1,) + ychunk)
+            found = [("y",)]
         if zform == "c":
-            buffer(f"rza_{i}", (half,) + zchunk)
-            buffer(f"rzb_{i}", (half - 1,) + zchunk)
-            buffer(f"sza_{i}", (half - 1,) + zchunk)
-            buffer(f"szb_{i}", (half - 2,) + zchunk)
-            found += [f"a{h}" for h in range(half)] + [f"b{h}" for h in range(half - 1)]
+            buffer(("rza", i), (half,) + zchunk)
+            buffer(("rzb", i), (half - 1,) + zchunk)
+            buffer(("sza", i), (half - 1,) + zchunk)
+            buffer(("szb", i), (half - 2,) + zchunk)
+            found += [("a", h) for h in range(half)] + [("b", h) for h in range(half - 1)]
         elif zform == "t":
-            buffer(f"rt_{i}", (7,) + zchunk)
-            buffer(f"st_{i}", (2,) + zchunk)
-            found += [f"t{h}" for h in range(7)]
+            buffer(("rt", i), (7,) + zchunk)
+            buffer(("st", i), (2,) + zchunk)
+            found += [("t", h) for h in range(7)]
         else:
-            buffer(f"rz_{i}", (nz - 1,) + zchunk)
-            found += ["z"]
+            buffer(("rz", i), (nz - 1,) + zchunk)
+            found += [("z",)]
         for n in found:
-            messages[f"{n}_{i}"] = len(messages)
+            messages[n + (i,)] = len(messages)
     for k, (c0, w, _) in enumerate(ROUNDS):
-        buffer(f"agg_{k}", (nb_all, strip, w))
-        buffer(f"stage_{k}", (n_dp, strip, w))
-        buffer(f"grad_{k}", (n_dp, strip, w))
+        buffer(("agg", k), (nb_all, strip, w))
+        buffer(("stage", k), (n_dp, strip, w))
+        buffer(("grad", k), (n_dp, strip, w))
     buffer("own", (nb_all, nz, NY, strip, width))
     buffer("lroot", (width, width))
     buffer("rroot", (width, width))
@@ -250,40 +247,40 @@
             first_y, first_z = yfirst, not yfirst
             ysize = kib * nz if yfirst else kib
             zsize = kib if yfirst else kib * NY
-            mid = buf[f"mid_{i}"]
+            mid = buf[("mid", i)]
             y_raw = own_y(g_ref if yfirst else mid)
             y_own = own_y(buf["own"] if yfirst else mid)
             z_raw = own_z(mid if yfirst else g_ref)
             z_own = own_z(mid if yfirst else buf["own"])
-            agg = buf[f"agg_{k}"].at[blocks]
-            ry1, ry2, ry3, sy = (buf.get(f"{n}_{i}") for n in ("ry1", "ry2", "ry3", "sy"))
-            rza, rzb, sza, szb = (buf.get(f"{n}_{i}") for n in ("rza", "rzb", "sza", "szb"))
-            ry, rz = buf.get(f"ry_{i}"), buf.get(f"rz_{i}")
-            rt, st = buf.get(f"rt_{i}"), buf.get(f"st_{i}")
+            agg = buf[("agg", k)].at[blocks]
+            ry1, ry2, ry3, sy = (buf.get((n, i)) for n in ("ry1", "ry2", "ry3", "sy"))
+            rza, rzb, sza, szb = (buf.get((n, i)) for n in ("rza", "rzb", "sza", "szb"))
+            ry, rz = buf.get(("ry", i)), buf.get(("rz", i))
+            rt, st = buf.get(("rt", i)), buf.get(("st", i))
             ylead = (yfirst, nz)
             zlead = (not yfirst, NY)
             up, down = s, -s
-            yl, zl = {1: f"y{s}", -1: f"y{-s}"}, {1: f"z{s}", -1: f"z{-s}"}
+            yl, zl = {1: ("y", s), -1: ("y", -s)}, {1: ("z", s), -1: ("z", -s)}
             yk, zk = (rank, k * 10 + 5) if yfirst else (k * 10 + 5, rank)
             yr, zr = (k * 10, zk) if yfirst else (yk, k * 10)
-            ybase = () if yfirst else (f"zdone_{i}",)
-            zbase = (f"ydone_{i}",) if yfirst else ()
+            ybase = () if yfirst else (("zd", i),)
+            zbase = (("yd", i),) if yfirst else ()
 
             def y0(i=i, y_raw=y_raw, ry1=ry1, ry3=ry3, s=s):
-                put(f"y1_{i}", y_raw(2 * s), ry1, ydev(s))
-                put(f"y3_{i}", y_raw(-s), ry3, ydev(-s))
+                put(("y1", i), y_raw(2 * s), ry1, ydev(s))
+                put(("y3", i), y_raw(-s), ry3, ydev(-s))
 
             def y1(i=i, k=k, y_own=y_own, ry1=ry1, ry2=ry2, sy=sy, s=s, fold=fold, ylead=ylead):
                 need_own(k)
-                copies[f"y1_{i}"].wait_recv()
+                copies[("y1", i)].wait_recv()
                 fold(sy, [ry1, y_own(s)], *ylead)
-                put(f"y2_{i}", sy, ry2, ydev(s))
+                put(("y2", i), sy, ry2, ydev(s))
 
             def y2(i=i, k=k, y_own=y_own, ry2=ry2, ry3=ry3, fold=fold, ylead=ylead,
                    dst=mid if yfirst else agg):
                 need_own(k)
-                copies[f"y2_{i}"].wait_recv()
-                copies[f"y3_{i}"].wait_recv()
+                copies[("y2", i)].wait_recv()
+                copies[("y3", i)].wait_recv()
                 fold(dst, [ry2, ry3, y_own(0)], *ylead)
 
             def straight(name, raw, into, far, dev):
@@ -296,98 +293,98 @@
                 copies[name] = Whole(into, send.at[i], recv.at[i])
 
             def ystart(i=i, y_raw=y_raw, ry=ry, straight=straight):
-                straight(f"y_{i}", y_raw, ry, YFAR, ydev)
+                straight(("y", i), y_raw, ry, YFAR, ydev)
 
             def yend(i=i, k=k, y_own=y_own, ry=ry, fold=fold, ylead=ylead, dst=mid if yfirst else agg):
                 need_own(k)
-                copies[f"y_{i}"].wait_recv()
+                copies[("y", i)].wait_recv()
                 fold(dst, [y_own(0)] + [ry.at[at] for at in range(NY - 1)], *ylead)
 
             def zflood(i=i, z_raw=z_raw, rz=rz, straight=straight):
-                straight(f"z_{i}", z_raw, rz, ZFAR, zdev)
+                straight(("z", i), z_raw, rz, ZFAR, zdev)
 
             def zsink(i=i, k=k, z_own=z_own, rz=rz, fold=fold, zlead=zlead, dst=agg if yfirst else mid):
                 need_own(k)
-                copies[f"z_{i}"].wait_recv()
+                copies[("z", i)].wait_recv()
                 fold(dst, [z_own(0)] + [rz.at[at] for at in range(nz - 1)], *zlead)
 
             def zpairs(i=i, z_raw=z_raw, rt=rt, s=s):
                 for at, (chunk, to) in enumerate(((4, 2), (3, 1), (-3, -1), (1, 1), (-1, -1))):
-                    put(f"t{at}_{i}", z_raw(chunk * s), rt.at[at], zdev(to * s))
+                    put(("t", at, i), z_raw(chunk * s), rt.at[at], zdev(to * s))
 
             def zjoin(i=i, k=k, z_own=z_own, rt=rt, st=st, s=s, fold=fold, zlead=zlead):
                 need_own(k)
                 for at in range(3):
-                    copies[f"t{at}_{i}"].wait_recv()
+                    copies[("t", at, i)].wait_recv()
                 fold(st.at[0], [rt.at[0], rt.at[1], z_own(2 * s)], *zlead)
-                put(f"t5_{i}", st.at[0], rt.at[5], zdev(2 * s))
+                put(("t", 5, i), st.at[0], rt.at[5], zdev(2 * s))
                 fold(st.at[1], [rt.at[2], z_own(-2 * s)], *zlead)
-                put(f"t6_{i}", st.at[1], rt.at[6], zdev(-2 * s))
+                put(("t", 6, i), st.at[1], rt.at[6], zdev(-2 * s))
 
             def zmeet(i=i, k=k, z_own=z_own, rt=rt, fold=fold, zlead=zlead, dst=agg if yfirst else mid):
                 need_own(k)
                 for at in range(3, 7):
-                    copies[f"t{at}_{i}"].wait_recv()
+                    copies[("t", at, i)].wait_recv()
                 fold(dst, [z_own(0)] + [rt.at[at] for at in range(3, 7)], *zlead)
 
             if yform == "c":
-                event(f"y0_{i}", y0, yk, after=ybase,
-                      sends=[(f"y1_{i}", yl[1], ysize), (f"y3_{i}", yl[-1], ysize)])
-                event(f"y1_{i}", y1, yr - 1, needs=[f"y1_{i}"], sends=[(f"y2_{i}", yl[1], ysize)], cost=0.1 + FOLD * ysize * 2)
-                event(f"ydone_{i}", y2, yr - 2, needs=[f"y2_{i}", f"y3_{i}"], cost=0.1 + FOLD * ysize * 3)
+                event(("y0", i), y0, yk, after=ybase,
+                      sends=[(("y1", i), yl[1], ysize), (("y3", i), yl[-1], ysize)])
+                event(("y1", i), y1, yr - 1, needs=[("y1", i)], sends=[(("y2", i), yl[1], ysize)], cost=0.1 + FOLD * ysize * 2)
+                event(("yd", i), y2, yr - 2, needs=[("y2", i), ("y3", i)], cost=0.1 + FOLD * ysize * 3)
             else:
-                event(f"y0_{i}", ystart, yk, after=ybase,
-                      sends=[(f"y+_{i}", yl[1], 2 * ysize), (f"y-_{i}", yl[-1], 2 * ysize)])
-                event(f"ydone_{i}", yend, yr - 2, needs=[f"y+_{i}", f"y-_{i}"], cost=0.1 + FOLD * ysize * 4)
+                event(("y0", i), ystart, yk, after=ybase,
+                      sends=[(("y+", i), yl[1], 2 * ysize), (("y-", i), yl[-1], 2 * ysize)])
+                event(("yd", i), yend, yr - 2, needs=[("y+", i), ("y-", i)], cost=0.1 + FOLD * ysize * 4)
             if zform == "t":
-                event(f"z0_{i}", zpairs, zk, after=zbase,
-                      sends=[(f"t+_{i}", zl[1], 3 * zsize), (f"t-_{i}", zl[-1], zsize),
-                             (f"T+_{i}", zl[1], zsize), (f"T-_{i}", zl[-1], zsize)])
-                event(f"z1_{i}", zjoin, zr - 1, needs=[f"t+_{i}", f"t-_{i}"],
-                      sends=[(f"u+_{i}", zl[1], 2 * zsize), (f"u-_{i}", zl[-1], 2 * zsize)], cost=0.2 + FOLD * zsize * 5)
-                event(f"zdone_{i}", zmeet, zr - 2, needs=[f"u+_{i}", f"u-_{i}", f"T+_{i}", f"T-_{i}"],
+                event(("z0", i), zpairs, zk, after=zbase,
+                      sends=[(("t+", i), zl[1], 3 * zsize), (("t-", i), zl[-1], zsize),
+                             (("T+", i), zl[1], zsize), (("T-", i), zl[-1], zsize)])
+                event(("z1", i), zjoin, zr - 1, needs=[("t+", i), ("t-", i)],
+                      sends=[(("u+", i), zl[1], 2 * zsize), (("u-", i), zl[-1], 2 * zsize)], cost=0.2 + FOLD * zsize * 5)
+                event(("zd", i), zmeet, zr - 2, needs=[("u+", i), ("u-", i), ("T+", i), ("T-", i)],
                       cost=0.1 + FOLD * zsize * 5)
             if zform == "d":
-                event(f"z0_{i}", zflood, zk, after=zbase,
-                      sends=[(f"z+_{i}", zl[1], 8 * zsize), (f"z-_{i}", zl[-1], 8 * zsize)])
-                event(f"zdone_{i}", zsink, zr - 2, needs=[f"z+_{i}", f"z-_{i}"], cost=0.1 + FOLD * zsize * 8)
+                event(("z0", i), zflood, zk, after=zbase,
+                      sends=[(("z+", i), zl[1], 8 * zsize), (("z-", i), zl[-1], 8 * zsize)])
+                event(("zd", i), zsink, zr - 2, needs=[("z+", i), ("z-", i)], cost=0.1 + FOLD * zsize * 8)
 
             def zstart(i=i, z_raw=z_raw, rza=rza, rzb=rzb, s=s):
-                put(f"a0_{i}", z_raw(half * s), rza.at[0], zdev(s))
-                put(f"b0_{i}", z_raw(-(half - 1) * s), rzb.at[0], zdev(-s))
+                put(("a", 0, i), z_raw(half * s), rza.at[0], zdev(s))
+                put(("b", 0, i), z_raw(-(half - 1) * s), rzb.at[0], zdev(-s))
 
             if zform == "c":
-                event(f"z0_{i}", zstart, zk, after=zbase,
-                      sends=[(f"a0_{i}", zl[1], zsize), (f"b0_{i}", zl[-1], zsize)])
+                event(("z0", i), zstart, zk, after=zbase,
+                      sends=[(("a", 0, i), zl[1], zsize), (("b", 0, i), zl[-1], zsize)])
                 for h in range(1, half):
                     def za(i=i, k=k, h=h, z_own=z_own, rza=rza, sza=sza, s=s, fold=fold, zlead=zlead):
                         need_own(k)
-                        copies[f"a{h - 1}_{i}"].wait_recv()
+                        copies[("a", h - 1, i)].wait_recv()
                         fold(sza.at[h - 1], [rza.at[h - 1], z_own((half - h) * s)], *zlead)
-                        put(f"a{h}_{i}", sza.at[h - 1], rza.at[h], zdev(s))
-
-                    event(f"za{h}_{i}", za, zr - 1, needs=[f"a{h - 1}_{i}"], sends=[(f"a{h}_{i}", zl[1], zsize)],
+                        put(("a", h, i), sza.at[h - 1], rza.at[h], zdev(s))
+
+                    event(("za", h, i), za, zr - 1, needs=[("a", h - 1, i)], sends=[(("a", h, i), zl[1], zsize)],
                           cost=0.1 + FOLD * zsize * 2)
                 for h in range(1, half - 1):
                     def zb(i=i, k=k, h=h, z_own=z_own, rzb=rzb, szb=szb, s=s, fold=fold, zlead=zlead):
                         need_own(k)
-                        copies[f"b{h - 1}_{i}"].wait_recv()
+                        copies[("b", h - 1, i)].wait_recv()
                         fold(szb.at[h - 1], [rzb.at[h - 1], z_own(-(half - 1 - h) * s)], *zlead)
-                        put(f"b{h}_{i}", szb.at[h - 1], rzb.at[h], zdev(-s))
-
-                    event(f"zb{h}_{i}", zb, zr - 1, needs=[f"b{h - 1}_{i}"], sends=[(f"b{h}_{i}", zl[-1], zsize)],
+                        put(("b", h, i), szb.at[h - 1], rzb.at[h], zdev(-s))
+
+                    event(("zb", h, i), zb, zr - 1, needs=[("b", h - 1, i)], sends=[(("b", h, i), zl[-1], zsize)],
                           cost=0.1 + FOLD * zsize * 2)
 
                 def zend(i=i, k=k, z_own=z_own, rza=rza, rzb=rzb, fold=fold, zlead=zlead,
                          dst=agg if yfirst else mid):
                     need_own(k)
-                    copies[f"a{half - 1}_{i}"].wait_recv()
-                    copies[f"b{half - 2}_{i}"].wait_recv()
+                    copies[("a", half - 1, i)].wait_recv()
+                    copies[("b", half - 2, i)].wait_recv()
                     fold(dst, [rza.at[half - 1], rzb.at[half - 2], z_own(0)], *zlead)
 
-                event(f"zdone_{i}", zend, zr - 2, needs=[f"a{half - 1}_{i}", f"b{half - 2}_{i}"],
+                event(("zd", i), zend, zr - 2, needs=[("a", half - 1, i), ("b", half - 2, i)],
                       cost=0.1 + FOLD * zsize * 3)
-            finals[k].append(f"zdone_{i}" if yfirst else f"ydone_{i}")
+            finals[k].append(("zd", i) if yfirst else ("yd", i))
 
         def block_of(device):
             found = jnp.int32(0)
@@ -404,7 +401,7 @@
             kib = strip * w * 2 / 1024
 
             def route(k=k):
-                agg, stage, grad = (buf[f"{n}_{k}"] for n in ("agg", "stage", "grad"))
+                agg, stage, grad = (buf[(n, k)] for n in ("agg", "stage", "grad"))
 
                 def one(o, _):
                     to = peer(o)
@@ -418,9 +415,9 @@
                 lax.fori_loop(1, n_dp, one, 0)
                 grad[me] = agg[block_of(me)]
 
-            event(f"route_{k}", route, k * 10 - 3, after=finals[k],
-                  sends=[(f"rz{q}_{k}", f"z{q}", kib * 8 * NY) for q in (1, -1)]
-                  + [(f"ry{q}_{k}", f"y{q}", kib * 2 * nz) for q in (1, -1)], cost=1.7)
+            event(("route", k), route, k * 10 - 3, after=finals[k],
+                  sends=[(("rz", q, k), ("z", q), kib * 8 * NY) for q in (1, -1)]
+                  + [(("ry", q, k), ("y", q), kib * 2 * nz) for q in (1, -1)], cost=1.7)
 
         def a2a_all(sem, ref):
             part = ref.at[pl.ds(0, n_dp - 1)]
@@ -429,13 +426,13 @@
         waited = []
 
         def land(k):
-            a2a_all(a2a_recv.at[k], buf[f"grad_{k}"]).wait()
+            a2a_all(a2a_recv.at[k], buf[("grad", k)]).wait()
             if not waited:
                 waited.append(k)
                 for c in loads:
                     c.wait()
             w = ROUNDS[k][1]
-            gk = buf[f"grad_{k}"][...].reshape(width, w)
+            gk = buf[("grad", k)][...].reshape(width, w)
             buf["half"][:, ROUNDS[k][0]:ROUNDS[k][0] + w] = jnp.dot(
                 buf["lroot"][...], gk, preferred_element_type=F32).astype(BF16)
             gf = gk.astype(F32)
@@ -443,8 +440,8 @@
             buf["gsq"][k] = sum(folded[:, c:c + 128] for c in range(0, w, 128))
 
         for k in range(n_rounds):
-            event(f"land_{k}", functools.partial(land, k), k * 10 - 4,
-                  needs=[f"rz{q}_{k}" for q in (1, -1)] + [f"ry{q}_{k}" for q in (1, -1)], cost=0.7)
+            event(("land", k), functools.partial(land, k), k * 10 - 4,
+                  needs=[("rz", q, k) for q in (1, -1)] + [("ry", q, k) for q in (1, -1)], cost=0.7)
 
         for c in own_copies:
             c.start()
@@ -460,7 +457,7 @@
 
 
         def whole():
-            parts = [buf[f"grad_{k}"][...].reshape(width, ROUNDS[k][1]) for k in range(n_rounds)]
+            parts = [buf[("grad", k)][...].reshape(width, ROUNDS[k][1]) for k in range(n_rounds)]
             return parts[0] if len(parts) == 1 else jnp.concatenate(parts, axis=1)
 
         owned = jnp.int32(0)
@@ -483,23 +480,6 @@
             p = jnp.dot(buf["half"][rows, :], buf["rroot"][...], preferred_element_type=F32)
             pre[pl.ds(i * per, per)] = p.astype(BF16).reshape(per, strip, width)
             squares = squares + jnp.sum((p * p).reshape(tall // 8, 8, width), axis=0)
-            if GIVE == "early":
-                def some(o, _, i=i):
-                    to = i * per + lax.rem(me + o, per)
-
-                    @pl.when(to != me)
-                    def _():
-                        give(to)
-
-                    return 0
-
-                lax.fori_loop(0, per, some, 0)
-        def give_to(spans):
-            for first, last in spans:
-                lax.fori_loop(first, last, lambda o, _: (give(peer(o)), 0)[1], 0)
-
-        if GIVE == "split":
-            give_to(FIRST)
         arrived[me] = pre[me]
 
         grad_squares = jnp.sum(buf["gsq"][...], axis=0)
@@ -535,18 +515,13 @@
 
         finish = exchange(buf["sum_t"], n_tensor, lambda o: (me, lax.rem(ten + o, n_tensor)), 0,
                           jnp.broadcast_to(share, (8, 128)))
-        if GIVE == "near":
-            lax.fori_loop(1, n_dp, lambda o, _: (give(peer(o)), 0)[1], 0)
-        if GIVE == "far":
-            lax.fori_loop(1, n_dp, lambda o, _: (give(peer(n_dp - o)), 0)[1], 0)
+        lax.fori_loop(1, n_dp, lambda o, _: (give(peer(o)), 0)[1], 0)
 
         lanes = lax.broadcasted_iota(jnp.int32, (8, 128), 1)
         in_row = lax.broadcasted_iota(jnp.int32, (8, 128), 0) == block
         local = jnp.where(lanes < 64, jnp.where(in_row, jnp.broadcast_to(factor, (8, 128)), 0.0), finish())
         finish = exchange(buf["sum_y"], NY, lambda o: (z * NY + lax.rem(y + o, NY), ten), 1, local)
         finish = exchange(buf["sum_z"], nz, lambda o: (lax.rem(z + o, nz) * NY + y, ten), 2, finish())
-        if GIVE == "split":
-            give_to(LAST)
 
         gram_weight = (1.0 - decay_rate) / width
 
@@ -559,7 +534,7 @@
             rows = pl.ds(i * tall, tall)
             gram = jnp.zeros((tall, width), F32)
             for k in range(n_rounds):
-                gk = buf[f"grad_{k}"]
+                gk = buf[("grad", k)]
                 per = tall // strip
                 top = gk[pl.ds(i * per, per)].reshape(tall, ROUNDS[k][1])
                 gram = gram + lax.dot_general(top, gk[...].reshape(width, ROUNDS[k][1]), (((1,), (1,)), ((), ())),
@@ -574,7 +549,7 @@
         for c in copies.values():
             c.wait_send()
         for k in range(n_rounds):
-            a2a_all(a2a_send.at[k], buf[f"stage_{k}"]).wait()
+            a2a_all(a2a_send.at[k], buf[("stage", k)]).wait()
 
         entries = nb_all * n_tensor * width * width
         norms = finish()

time: 72.3 us -> 72.3 us (level)
  no operation moved by 1% of the time
where the time goes in v4:
time: 72.3 us; the launch traced here: 71.7 us
  Pallas kernels  68.5 us (95%)
  local copies, waits for them, and re-layouts  2.6 us (4%)
    pallas_call x1, Pallas kernels, per_device(): pl.pallas_call(kernel, out_shape=(pltpu.VMEM((width, width), F32), pltpu....  68.5 us
    unnamed x3, local copies, waits for them, and re-layouts  2.6 us

profile of v4, /device:TPU:32, one launch (start us, length us, event | category | flops | bytes accessed | tf_op | source)
XLA Modules:
  0.0 71.7 jit_solution(17039445688104847774)
XLA Ops:
  0.6 68.5 %shampoo.1 = (f32[512,512]{1,0:T(8,128)S(1)}, f32[512,512]{1,0:T(8,128)S(1)}, bf16[8,16,512]{2,1,0:T(8,128)(2,1)S(1)}) custom-call(s32[1,32]{1,0:T(1,128)} %owners_ref.1, bf16[8,8,4,16,512]{4,3,2,1,0:T(8,128)(2,1)} %bitcast.9, f32[512,512]{1,0:T(8,128)} %bitcast.10, f32[512,512]{1,0:T(8,128)} %bitcast.11, bf16[512,512]{1,0:T(8,128)(2,1)} %bitcast.12, ...), custom_call_target="tpu_custom_call" | custom-call | tf_op jit(solution)/shard_map/shampoo/pallas_call | solution.py:570
  69.1 1.0 %copy.12 = f32[1,1,512,512]{3,2,1,0:T(8,128)} copy(f32[1,1,512,512]{3,2,1,0:T(8,128)S(1)} %bitcast.8) | data formatting | bytes 2097152
  70.1 1.0 %copy.13 = f32[1,1,512,512]{3,2,1,0:T(8,128)} copy(f32[1,1,512,512]{3,2,1,0:T(8,128)S(1)} %bitcast.7) | data formatting | bytes 2097152
  71.0 0.7 copy.14

commit v5 on v4

--- a/solution.py
+++ b/solution.py
@@ -15,28 +15,27 @@
 NY = 4
 
 ROUNDS = (
-    (0, 128, (
-        (4, "y", 1, "ct", 13.1),
-        (3, "y", -1, "cc", 6.5),
-        (1, "z", 1, "cd", 7.2),
+    (0, 256, (
+        (1, "y", 1, "cd", -6.07),
+        (3, "y", -1, "ct", 8.4),
+        (3, "y", 1, "ct", 11.2),
+        (1, "z", 1, "cd", -1.16),
     )),
-    (128, 256, (
-        (2, "y", -1, "ct", 15.8),
-        (3, "z", 1, "cd", 12.0),
-        (2, "z", -1, "cd", 21.6),
-        (1, "y", 1, "cd", 16.8),
+    (256, 128, (
+        (3, "z", -1, "cd", 14.79),
+        (5, "z", 1, "cd", 12.9),
     )),
     (384, 128, (
-        (4, "y", -1, "cd", 29.3),
-        (3, "z", 1, "cd", 19.8),
-        (1, "y", 1, "cd", 21.2),
+        (5, "z", -1, "cd", 25.3),
+        (2, "y", -1, "cd", 11.75),
+        (1, "y", -1, "cd", 27.9),
     )),
 )
 FULL = False
 FOLD = 0.002
 YFAR = (1, -1, 2)
 ZFAR = (1, -1, 2, -2, 3, -3, 4)
-MODEL = (46.5, 2.2, 3.0)
+MODEL = (47.5, 2.0, 3.0)
 
 
 class Whole:
@@ -134,6 +133,7 @@
     buffer("rfac", (width, width), F32)
     buffer("pre", (n_dp, strip, width))
     buffer("half", (width, width))
+    buffer("turned", (width, width))
     buffer("gsq", (len(ROUNDS), 8, 128), F32)
     buffer("arrived", (n_dp, strip, width))
     buffer("sum_t", (n_tensor, 8, 128), F32)
@@ -530,22 +530,28 @@
             add = lax.select(mine, add, jnp.zeros_like(add))
             return decay_rate * factor_ref + add
 
-        for i in range(width // tall):
+        grad = whole()
+        flipped = grad.T
+        buf["turned"][...] = flipped
+
+        def left_rows(i, _):
             rows = pl.ds(i * tall, tall)
             gram = jnp.zeros((tall, width), F32)
-            for k in range(n_rounds):
-                gk = buf[("grad", k)]
-                per = tall // strip
-                top = gk[pl.ds(i * per, per)].reshape(tall, ROUNDS[k][1])
-                gram = gram + lax.dot_general(top, gk[...].reshape(width, ROUNDS[k][1]), (((1,), (1,)), ((), ())),
-                                              preferred_element_type=F32)
+            for k, (c0, w, _) in enumerate(ROUNDS):
+                top = buf[("grad", k)][pl.ds(i * per, per)].reshape(tall, w)
+                gram = gram + jnp.dot(top, buf["turned"][c0:c0 + w, :], preferred_element_type=F32)
             nl_ref[rows, :] = statistic(buf["lfac"][rows, :], gram)
-        grad = whole()
-        flipped = grad.T
-        for i in range(width // tall):
+            return 0
+
+        lax.fori_loop(0, width // tall, left_rows, 0)
+        def right_rows(i, _):
             rows = pl.ds(i * tall, tall)
-            gram = jnp.dot(flipped[i * tall:(i + 1) * tall], grad, preferred_element_type=F32)
-            nr_ref[rows, :] = statistic(buf["rfac"][rows, :], gram)
+            for k, (c0, w, _) in enumerate(ROUNDS):
+                gram = jnp.dot(buf["turned"][rows, :], buf[("grad", k)][...].reshape(width, w), preferred_element_type=F32)
+                nr_ref[rows, c0:c0 + w] = statistic(buf["rfac"][rows, c0:c0 + w], gram)
+            return 0
+
+        lax.fori_loop(0, width // tall, right_rows, 0)
         for c in copies.values():
             c.wait_send()
         for k in range(n_rounds):

time: 72.3 us -> 71.3 us (0.986)
  no operation moved by 1% of the time
where the time goes in v5:
time: 71.3 us; the launch traced here: 71 us
  Pallas kernels  67.8 us (95%)
  local copies, waits for them, and re-layouts  2.6 us (4%)
    pallas_call x1, Pallas kernels, per_device(): pl.pallas_call(kernel, out_shape=(pltpu.VMEM((width, width), F32), pltpu....  67.8 us
    unnamed x3, local copies, waits for them, and re-layouts  2.6 us

profile of v5, /device:TPU:32, one launch (start us, length us, event | category | flops | bytes accessed | tf_op | source)
XLA Modules:
  0.0 71.0 jit_solution(2764739718607451472)
XLA Ops:
  0.6 67.8 %shampoo.1 = (f32[512,512]{1,0:T(8,128)S(1)}, f32[512,512]{1,0:T(8,128)S(1)}, bf16[8,16,512]{2,1,0:T(8,128)(2,1)S(1)}) custom-call(s32[1,32]{1,0:T(1,128)} %owners_ref.1, bf16[8,8,4,16,512]{4,3,2,1,0:T(8,128)(2,1)} %bitcast.9, f32[512,512]{1,0:T(8,128)} %bitcast.10, f32[512,512]{1,0:T(8,128)} %bitcast.11, bf16[512,512]{1,0:T(8,128)(2,1)} %bitcast.12, ...), custom_call_target="tpu_custom_call" | custom-call | tf_op jit(solution)/shard_map/shampoo/pallas_call | solution.py:576
  68.4 1.0 %copy.12 = f32[1,1,512,512]{3,2,1,0:T(8,128)} copy(f32[1,1,512,512]{3,2,1,0:T(8,128)S(1)} %bitcast.8) | data formatting | bytes 2097152
  69.4 1.0 %copy.13 = f32[1,1,512,512]{3,2,1,0:T(8,128)} copy(f32[1,1,512,512]{3,2,1,0:T(8,128)S(1)} %bitcast.7) | data formatting | bytes 2097152
  70.4 0.7 copy.14

commit v6 on v5

--- a/solution.py
+++ b/solution.py
@@ -19,18 +19,20 @@
         (1, "y", 1, "cd", -6.07),
         (3, "y", -1, "ct", 8.4),
         (3, "y", 1, "ct", 11.2),
-        (1, "z", 1, "cd", -1.16),
+        (1, "z", 1, "cd", -6.03),
     )),
     (256, 128, (
-        (3, "z", -1, "cd", 14.79),
+        (3, "z", -1, "cd", 19.4),
         (5, "z", 1, "cd", 12.9),
     )),
     (384, 128, (
         (5, "z", -1, "cd", 25.3),
-        (2, "y", -1, "cd", 11.75),
-        (1, "y", -1, "cd", 27.9),
+        (1, "y", -1, "cd", 13.09),
+        (2, "y", -1, "cd", 19.2),
     )),
 )
+FIRST = ((4, 32),)
+LAST = ((1, 4),)
 FULL = False
 FOLD = 0.002
 YFAR = (1, -1, 2)
@@ -515,13 +517,18 @@
 
         finish = exchange(buf["sum_t"], n_tensor, lambda o: (me, lax.rem(ten + o, n_tensor)), 0,
                           jnp.broadcast_to(share, (8, 128)))
-        lax.fori_loop(1, n_dp, lambda o, _: (give(peer(o)), 0)[1], 0)
+        def give_to(spans):
+            for first, last in spans:
+                lax.fori_loop(first, last, lambda o, _: (give(peer(o)), 0)[1], 0)
+
+        give_to(FIRST)
 
         lanes = lax.broadcasted_iota(jnp.int32, (8, 128), 1)
         in_row = lax.broadcasted_iota(jnp.int32, (8, 128), 0) == block
         local = jnp.where(lanes < 64, jnp.where(in_row, jnp.broadcast_to(factor, (8, 128)), 0.0), finish())
         finish = exchange(buf["sum_y"], NY, lambda o: (z * NY + lax.rem(y + o, NY), ten), 1, local)
         finish = exchange(buf["sum_z"], nz, lambda o: (lax.rem(z + o, nz) * NY + y, ten), 2, finish())
+        give_to(LAST)
 
         gram_weight = (1.0 - decay_rate) / width
 

time: 71.3 us -> 70.9 us (level)
  no operation moved by 1% of the time
where the time goes in v6:
time: 70.9 us
  Pallas kernels  67.6 us (95%)
  local copies, waits for them, and re-layouts  2.6 us (4%)
    pallas_call x1, Pallas kernels, per_device(): pl.pallas_call(kernel, out_shape=(pltpu.VMEM((width, width), F32), pltpu....  67.6 us
    unnamed x3, local copies, waits for them, and re-layouts  2.6 us

profile of v6, /device:TPU:32, one launch (start us, length us, event | category | flops | bytes accessed | tf_op | source)
XLA Modules:
  0.0 70.9 jit_solution(16454051237749734004)
XLA Ops:
  0.6 67.6 %shampoo.1 = (f32[512,512]{1,0:T(8,128)S(1)}, f32[512,512]{1,0:T(8,128)S(1)}, bf16[8,16,512]{2,1,0:T(8,128)(2,1)S(1)}) custom-call(s32[1,32]{1,0:T(1,128)} %owners_ref.1, bf16[8,8,4,16,512]{4,3,2,1,0:T(8,128)(2,1)} %bitcast.9, f32[512,512]{1,0:T(8,128)} %bitcast.10, f32[512,512]{1,0:T(8,128)} %bitcast.11, bf16[512,512]{1,0:T(8,128)(2,1)} %bitcast.12, ...), custom_call_target="tpu_custom_call" | custom-call | tf_op jit(solution)/shard_map/shampoo/pallas_call | solution.py:583
  68.3 1.0 %copy.12 = f32[1,1,512,512]{3,2,1,0:T(8,128)} copy(f32[1,1,512,512]{3,2,1,0:T(8,128)S(1)} %bitcast.8) | data formatting | bytes 2097152
  69.2 1.0 %copy.13 = f32[1,1,512,512]{3,2,1,0:T(8,128)} copy(f32[1,1,512,512]{3,2,1,0:T(8,128)S(1)} %bitcast.7) | data formatting | bytes 2097152
  70.2 0.7 copy.14

commit v7 on v6

--- a/solution.py
+++ b/solution.py
@@ -445,9 +445,9 @@
             event(("land", k), functools.partial(land, k), k * 10 - 4,
                   needs=[("rz", q, k) for q in (1, -1)] + [("ry", q, k) for q in (1, -1)], cost=0.7)
 
+        greet()
         for c in own_copies:
             c.start()
-        greet()
         order, _ = plan(events, *MODEL)
         started = False
         for e in order:

time: 70.9 us -> 72.3 us (1.020)
  Pallas kernels: 67.6 us -> 69 us
    pallas_call x1, Pallas kernels: 67.6 us -> 69 us  [per_device(): pl.pallas_call(kernel, out_shape=(pltpu.VMEM((width, width), F32), pltpu....]
where the time goes in v7:
time: 72.3 us; the launch traced here: 72.2 us
  Pallas kernels  69 us (95%)
  local copies, waits for them, and re-layouts  2.6 us (4%)
    pallas_call x1, Pallas kernels, per_device(): pl.pallas_call(kernel, out_shape=(pltpu.VMEM((width, width), F32), pltpu....  69 us
    unnamed x3, local copies, waits for them, and re-layouts  2.6 us

profile of v7, /device:TPU:32, one launch (start us, length us, event | category | flops | bytes accessed | tf_op | source)
XLA Modules:
  0.0 72.2 jit_solution(4716872953701541410)
XLA Ops:
  0.6 69.0 %shampoo.1 = (f32[512,512]{1,0:T(8,128)S(1)}, f32[512,512]{1,0:T(8,128)S(1)}, bf16[8,16,512]{2,1,0:T(8,128)(2,1)S(1)}) custom-call(s32[1,32]{1,0:T(1,128)} %owners_ref.1, bf16[8,8,4,16,512]{4,3,2,1,0:T(8,128)(2,1)} %bitcast.9, f32[512,512]{1,0:T(8,128)} %bitcast.10, f32[512,512]{1,0:T(8,128)} %bitcast.11, bf16[512,512]{1,0:T(8,128)(2,1)} %bitcast.12, ...), custom_call_target="tpu_custom_call" | custom-call | tf_op jit(solution)/shard_map/shampoo/pallas_call | solution.py:583
  69.7 1.0 %copy.12 = f32[1,1,512,512]{3,2,1,0:T(8,128)} copy(f32[1,1,512,512]{3,2,1,0:T(8,128)S(1)} %bitcast.8) | data formatting | bytes 2097152
  70.6 1.0 %copy.13 = f32[1,1,512,512]{3,2,1,0:T(8,128)} copy(f32[1,1,512,512]{3,2,1,0:T(8,128)S(1)} %bitcast.7) | data formatting | bytes 2097152
  71.6 0.7 copy.14
